TPU v7x, 128 devices: a whole 4x4x4 slice. The times are simulated.
128 devices in a mesh: dp: 4 (over x), vocab: 32 (over z, y, core).
Axes of the slice: x: 4, y: 4, z: 4, core: 2. Of those that a mesh axis runs over, the one named last changes fastest.
Arguments:
- hidden: bfloat16 [1024, 2304], P('dp', 'vocab'), may hold values from -6 to 6
- embed: bfloat16 [128000, 2304], P('vocab')
- token_ids: int32 [1024], P('dp'), may hold values from 0 to 127999
- lookup_cot: bfloat16 [1024, 2304], P('dp', 'vocab'), may hold values from -0.15625 to 0.15625
- teacher_ids: int32 [1024, 64], P(('dp', 'vocab')), may hold values from 0 to 127999, as said below
- teacher_logits: float32 [1024, 64], P(('dp', 'vocab')), may hold values from -8 to 8
Outputs:
- hidden_grad: bfloat16 [1024, 2304], P('dp', 'vocab')
- embed_grad: bfloat16 [128000, 2304], P('vocab', 'dp')
- divergence: float32 [1024], P(('dp', 'vocab'))
Inputs may be any that keep to these rules, and one draw needn't show every extreme that they name: `teacher_ids`: each token's 64 teacher ids are different.
All inputs are finite; a program needn't handle non-finite values.
Results may differ from a plain program's by a relative error of at most 0.0043.
The roundings to bfloat16 on the way count: a program that leaves them out, or rounds other values in their place, can miss the bound.
Values may be sent and summed in bfloat16 or wider, within the bound.
No kernel may reach another device: no remote copies, remote signals or barrier semaphores. Data moves between devices by JAX's collectives and lax.ppermute only.
A program may use at most 192 MiB of HBM per device.

v0:
```python
import functools
import math

import jax
import jax.numpy as jnp
from jax import lax
from jax.experimental import pallas as pl
from jax.experimental.pallas import tpu as pltpu
from jax.sharding import Mesh, PartitionSpec as P

SOFT_CAP = 30.0
LOSS_SCALE = 16.0
BLOCK = 256
HALF = 128
ROW_TILE = 400
ROW_STEP = 800
LONG_STEP = 2000
PADDED = 4096
STRIP = 16
GRAD_TILE = 512
TABLE_TILE = 256
FAST_SLOTS = 4
HIDDEN_SLOTS = 5
FAR = 1 << 30
LOG2_E = math.log2(math.e)
RING = ("z", "y", "core")
EVERY = ("dp",) + RING
SIDE = 4
OFFSETS = (0, 1, 3, 2)


def dot_nn(a, b):
    return lax.dot_general(a, b, (((1,), (0,)), ((), ())), preferred_element_type=jnp.float32)


def dot_nt(a, b):
    return lax.dot_general(a, b, (((1,), (1,)), ((), ())), preferred_element_type=jnp.float32)


def dot_tn(a, b):
    return lax.dot_general(a, b, (((0,), (0,)), ((), ())), preferred_element_type=jnp.float32)


def offset_of(index, core):
    return jnp.where(core == 0, OFFSETS[index], OFFSETS[(0, 2, 1, 3)[index]])


def chip_of(outer, inner, core, z, y):
    first, second = OFFSETS[inner], OFFSETS[outer]
    row = lax.rem(z + jnp.where(core == 0, second, first), SIDE)
    column = lax.rem(y + jnp.where(core == 0, first, second), SIDE)
    return row * SIDE + column


def here():
    return tuple(lax.axis_index(name) for name in EVERY)


def block_offset(rows, z, y, core):
    return ((z * SIDE + y) * 2 + core) * rows


def teacher_kernel(rows, thin, near, far, cot, ids, prob, row_counts, column_counts, joined):
    _, z, y, core = here()
    offset = block_offset(rows, z, y, core)
    top = ids.shape[1]
    share = 8
    group = thin + 2 * share
    for side, source in ((core, near), (1 - core, far)):
        lanes = pl.ds(pl.multiple_of(side * HALF, HALF), HALF)
        for outer in range(SIDE):
            for inner in range(SIDE):
                chip = chip_of(outer, inner, side, z, y)
                for other in range(2):
                    start = ((outer * SIDE + inner) * 2 + other) * group
                    rank = chip * 2 + other
                    into = pl.multiple_of(rank * thin, 8)
                    cot[pl.ds(into, thin), lanes] = source[start : start + thin]
                    for half in range(2):
                        held = source[start + thin + half * share : start + thin + (half + 1) * share]
                        joined[side * 2 + half, pl.ds(pl.multiple_of(rank * share, 8), share)] = held
    for block in range(SIDE):
        flipped = joined[offset_of(block, core)].T
        scores = flipped[:top]
        local = flipped[top:].astype(jnp.int32) - offset
        raised = jnp.exp(scores - jnp.max(scores, axis=0, keepdims=True))
        ids[block] = local
        prob[block] = raised / jnp.sum(raised, axis=0, keepdims=True)
        size = GRAD_TILE if block == 0 else TABLE_TILE
        for tile in range(PADDED // size):
            first = tile * size
            inside = (local >= first) & (local < min(first + size, rows))
            most = jnp.max(jnp.sum(inside.astype(jnp.int32), axis=0))
            if block == 0:
                row_counts[tile] = most
            else:
                column_counts[tile * (SIDE - 1) + block - 1] = most


def lookup_kernel(rows, share, packs, cot, packed_cot, packed_ids, chunks, tokens):
    mine, z, y, core = here()
    offset = block_offset(rows, z, y, core)
    count = tokens.shape[1]
    blocks = count // BLOCK
    for index in range(blocks):
        start = lax.rem(mine + OFFSETS[index], blocks) * BLOCK
        for half in range(BLOCK // HALF):
            lanes = pl.ds(pl.multiple_of(start + half * HALF, HALF), HALF)
            tokens[:, lanes] = packs[index, share + half : share + half + 1]
    local = tokens[...].astype(jnp.int32) - offset
    inside = (local >= 0) & (local < rows)
    hit = jnp.broadcast_to(jnp.where(inside, 1.0, 0.0), (8, count))
    before = lax.broadcasted_iota(jnp.int32, (count, count), 0)
    after = lax.broadcasted_iota(jnp.int32, (count, count), 1)
    upto = jnp.where(before <= after, 1.0, 0.0).astype(jnp.bfloat16)
    running = dot_nn(hit.astype(jnp.bfloat16), upto)[0:1].astype(jnp.int32)
    rank = jnp.where(inside, running - 1, -1)
    total = jnp.max(running)
    chunks[0] = (total + BLOCK - 1) // BLOCK
    safe = jnp.where(inside, local, 0)
    high = jnp.broadcast_to((safe >> 6).astype(jnp.float32), (8, count)).astype(jnp.bfloat16)
    low = jnp.broadcast_to((safe & 63).astype(jnp.float32), (8, count)).astype(jnp.bfloat16)
    for chunk in range(blocks):

        @pl.when(chunk * BLOCK < jnp.maximum(total, 1))
        def _():
            slot = lax.broadcasted_iota(jnp.int32, (BLOCK, count), 0) + chunk * BLOCK
            chosen = jnp.where(slot == rank, 1.0, 0.0).astype(jnp.bfloat16)
            columns = cot.shape[0] // blocks
            taken = jnp.zeros((columns, BLOCK), jnp.float32)
            for block in range(blocks):
                span = slice(block * BLOCK, (block + 1) * BLOCK)
                part = cot[block * columns : (block + 1) * columns].astype(jnp.bfloat16)
                taken = taken + dot_nt(part, chosen[:, span])
            packed_cot[chunk] = taken.astype(jnp.bfloat16)
            row = dot_nt(high, chosen)[0:1] * 64.0 + dot_nt(low, chosen)[0:1]
            used = dot_nt(hit.astype(jnp.bfloat16), chosen)[0:1] > 0.5
            packed_ids[chunk] = jnp.where(used, row.astype(jnp.int32), -1)


def next_slot(relative, prob, last):
    following = jnp.min(jnp.where(relative > last, relative, FAR), axis=0, keepdims=True)
    chance = jnp.sum(jnp.where(relative == following, prob, 0.0), axis=0, keepdims=True)
    return following, chance


def join_halves(near, far, joined):
    _, z, y, core = here()
    pair = near.shape[0] // (SIDE * SIDE)
    for side, source in ((core, near), (1 - core, far)):
        lanes = pl.ds(pl.multiple_of(side * HALF, HALF), HALF)
        for outer in range(SIDE):
            for inner in range(SIDE):
                start = (outer * SIDE + inner) * pair
                into = pl.multiple_of(chip_of(outer, inner, side, z, y) * pair, 16)
                joined[pl.ds(into, pair), lanes] = source[start : start + pair]


def table_copy(step, table, held, ready):
    rows = pl.ds(pl.multiple_of(step * ROW_STEP, STRIP), ROW_STEP)
    return pltpu.make_async_copy(table.at[rows], held.at[rows], ready.at[step])


def logit_kernel(blocks, fresh, embed, *refs):
    near, far = refs[:blocks], refs[blocks : 2 * blocks]
    squashed, total, columns = refs[2 * blocks : 2 * blocks + 3]
    rest = refs[2 * blocks + 3 :]
    step = pl.program_id(0)
    steps = pl.num_programs(0)
    length = ROW_STEP if fresh else LONG_STEP
    if fresh:
        held, hidden, sums, ready = rest

        @pl.when(step == 0)
        def _():
            for index in range(embed.shape[0] // ROW_STEP):
                table_copy(index, embed, held, ready).start()
            rows = embed.shape[0]
            held[rows:] = jnp.zeros((PADDED - rows, held.shape[1]), held.dtype)

    else:
        held, (hidden, sums) = embed, rest

    @pl.when(step == 0)
    def _():
        sums[...] = jnp.zeros_like(sums)
        used = ROW_STEP * (PADDED // ROW_STEP)
        squashed[used:] = jnp.zeros((PADDED - used, squashed.shape[1]), jnp.float32)
        size = columns.shape[1]
        start = pl.multiple_of(lax.axis_index("dp") * size, 16)
        for block in range(blocks):
            join_halves(near[block], far[block], hidden.at[block])
            columns[block] = hidden[block, pl.ds(start, size)]

    if fresh:
        table_copy(step, embed, held, ready).wait()

    for first in range(0, length, ROW_TILE):
        from_table = pl.ds(pl.multiple_of(step * length + first, STRIP), ROW_TILE)
        for block in range(blocks):
            span = slice(block * BLOCK, (block + 1) * BLOCK)
            raw = dot_nn(held[from_table], hidden[block])
            raised = jnp.zeros((8, BLOCK), jnp.float32)
            for chunk in range(0, ROW_TILE, STRIP):
                ratio = jnp.tanh(raw[chunk : chunk + STRIP] * (1.0 / SOFT_CAP))
                into = pl.multiple_of(step * length + first + chunk, STRIP)
                squashed[pl.ds(into, STRIP), span] = ratio
                power = jnp.exp2(ratio * (SOFT_CAP * LOG2_E))
                raised = raised + (power[:8] + power[8:])
            sums[:, span] += raised

    @pl.when(step == steps - 1)
    def _():
        total[...] = jnp.sum(sums[...], axis=0, keepdims=True)


def gradient(ratio, target, log_share):
    share = jnp.exp2(ratio * (SOFT_CAP * LOG2_E) + log_share)
    return (share - target) * (1.0 - ratio * ratio)


def logit_grads(squashed, grads, log_share, relative, chances, fast, term=None):
    last = jnp.full((1, BLOCK), -1, jnp.int32)
    slots = []
    for _ in range(fast):
        last, chance = next_slot(relative, chances, last)
        slots.append((last, chance * LOSS_SCALE))
    row = lax.broadcasted_iota(jnp.int32, (STRIP, BLOCK), 0)
    added = jnp.zeros((8, BLOCK), jnp.float32)
    for start in range(0, grads.shape[0], STRIP):
        strip = slice(start, start + STRIP)
        ratio = squashed[strip]
        target = jnp.zeros((STRIP, BLOCK), jnp.float32)
        for where, value in slots:
            target = jnp.where(row + start == where, value, target)
        grads[strip] = gradient(ratio, target, log_share).astype(jnp.bfloat16)
        if term is not None:
            product = target * ratio
            added = added + (product[:8] + product[8:])
    if term is not None:
        term[...] += added
    return last


def more_targets(
    squashed, grads, log_share, relative, chances, last, fast, count, term=None
):
    row = lax.broadcasted_iota(jnp.int32, (STRIP, BLOCK), 0)

    def slot(_, last):
        last, chance = next_slot(relative, chances, last)
        value = chance * LOSS_SCALE

        def strip(index, _):
            start = pl.multiple_of(index * STRIP, STRIP)
            rows = pl.ds(start, STRIP)
            ratio = squashed[rows]
            hit = row + start == last
            fresh = gradient(ratio, jnp.broadcast_to(value, ratio.shape), log_share)
            held = grads[rows].astype(jnp.float32)
            grads[rows] = jnp.where(hit, fresh, held).astype(jnp.bfloat16)
            if term is not None:
                product = jnp.where(hit, value * ratio, 0.0)
                term[...] += product[:8] + product[8:]
            return 0

        lax.fori_loop(0, grads.shape[0] // STRIP, strip, 0)
        return last

    lax.fori_loop(fast, count, slot, last)


def hidden_grad_kernel(
    counts,
    embed,
    squashed,
    total,
    ids,
    prob,
    grads,
    keep,
    give,
    rows_grad,
    flipped,
    term,
    ready,
    made,
):
    width = embed.shape[1]
    log_share = jnp.log2(LOSS_SCALE / total[:, 0:BLOCK])
    term[...] = jnp.zeros_like(term)
    ready[...] = jnp.zeros_like(ready)
    rows_grad[...] = jnp.zeros_like(rows_grad)
    tiles = PADDED // GRAD_TILE

    def rows_of(tile):
        return pl.ds(pl.multiple_of(tile * GRAD_TILE, GRAD_TILE), GRAD_TILE)

    def step(tile, _):
        rows = rows_of(tile)
        rows_grad[...] += dot_tn(ready[...], embed[rows_of(jnp.maximum(tile - 1, 0))])
        held = squashed.at[rows]
        relative = ids[0] - tile * GRAD_TILE
        last = logit_grads(held, made, log_share, relative, prob[0], HIDDEN_SLOTS, term)

        @pl.when(counts[tile] > HIDDEN_SLOTS)
        def _():
            more_targets(
                held,
                made,
                log_share,
                ids[0] - tile * GRAD_TILE,
                prob[0],
                last,
                HIDDEN_SLOTS,
                counts[tile],
                term,
            )

        ready[...] = made[...]
        grads[rows] = made[...]
        return 0

    lax.fori_loop(0, tiles, step, 0)
    rows_grad[...] += dot_tn(ready[...], embed[rows_of(tiles - 1)])

    _, z, y, core = here()
    thin = keep.shape[2] - 8
    for part in range(width // BLOCK):
        span = slice(part * BLOCK, (part + 1) * BLOCK)
        flipped[span, :] = rows_grad[:, span].T
    summed = jnp.sum(term[...], axis=0, keepdims=True) * (SOFT_CAP / LOSS_SCALE)
    for outer in range(SIDE):
        for inner in range(SIDE):
            for ref, side in ((keep, core), (give, 1 - core)):
                rank = 2 * chip_of(outer, inner, side, z, y) + side
                start = pl.multiple_of(rank * thin, 8)
                ref[outer, inner, 0:thin] = flipped[pl.ds(start, thin)]
                ref[outer, inner, thin : thin + 8] = jnp.broadcast_to(summed, (8, BLOCK))


def halve_kernel(keep, got, *outs):
    for index, out in enumerate(outs):
        out[...] = keep[index] + got[index]


def quarter_kernel(*refs):
    parts, outs = refs[:SIDE], refs[SIDE:]
    for index, out in enumerate(outs):
        out[...] = (parts[0][index] + parts[1][index]) + (parts[2][index] + parts[3][index])


def finish_kernel(total, teacher_logits, *refs):
    parts, (hidden_grad, divergence) = refs[:SIDE], refs[SIDE:]
    _, z, y, core = here()
    summed = (parts[0][...] + parts[1][...]) + (parts[2][...] + parts[3][...])
    thin = hidden_grad.shape[0]
    hidden_grad[...] = summed[:thin].astype(jnp.bfloat16)
    scores = teacher_logits[...]
    share = scores.shape[0]
    shifted = scores - jnp.max(scores, axis=1, keepdims=True)
    raised = jnp.exp(shifted)
    prob = raised / jnp.sum(raised, axis=1, keepdims=True)
    entropy = jnp.sum(prob * jnp.log(prob), axis=1, keepdims=True)
    rest = jnp.log(total[:, 0:BLOCK]) - summed[thin : thin + 1]
    first = ((z * SIDE + y) * 2 + core) * share
    lane = lax.broadcasted_iota(jnp.int32, (share, BLOCK), 1)
    token = lax.broadcasted_iota(jnp.int32, (share, BLOCK), 0) + first
    value = entropy + jnp.sum(jnp.where(lane == token, rest, 0.0), axis=1, keepdims=True)
    line = lax.broadcasted_iota(jnp.int32, (share, HALF), 0)
    column = lax.broadcasted_iota(jnp.int32, (share, HALF), 1)
    divergence[...] = jnp.sum(jnp.where(line == column, value, 0.0), axis=0, keepdims=True)


def table_grad_kernel(
    width,
    fresh,
    counts,
    chunks,
    own_grads,
    side_squashed,
    far_squashed,
    total,
    ids,
    prob,
    packed_cot,
    packed_ids,
    own_columns,
    side_columns,
    far_columns,
    *refs,
):
    blocks = SIDE - 1
    tiles = PADDED // TABLE_TILE // 2
    first = 0 if fresh else tiles
    out, left, ready, made = refs[-4:]
    now = pl.program_id(0) == pl.num_programs(0) - 1

    if not fresh:

        @pl.when(jnp.logical_not(now))
        def _():
            out[...] = refs[0][...]

    def rows_of(tile):
        return pl.ds(pl.multiple_of(tile * TABLE_TILE, TABLE_TILE), TABLE_TILE)

    def onehot(tile, chunk):
        column = lax.broadcasted_iota(jnp.int32, (TABLE_TILE, BLOCK), 0) + tile * TABLE_TILE
        chosen = jnp.where(column == packed_ids[chunk], math.sqrt(width), 0.0)
        return chosen.astype(jnp.bfloat16)

    def product():
        return dot_nt(left[...], ready[...])

    def put(index, value):
        out[:, rows_of(index)] = value.astype(jnp.bfloat16)

    def more_lookups(index):
        spread = lax.fori_loop(
            1,
            chunks[0],
            lambda chunk, held: held + dot_nt(packed_cot[chunk], onehot(first + index, chunk)),
            product(),
        )
        put(index, spread)

    def step(index, _):
        tile = first + index
        rows = rows_of(tile)
        before = jnp.maximum(index - 1, 0)
        put(before, product())
        made[:, 0:BLOCK] = own_grads[rows]
        made[:, 4 * BLOCK :] = onehot(tile, 0)

        def of(block):
            lanes = pl.ds(block * BLOCK, BLOCK)
            held = far_squashed.at[rows] if block == 2 else side_squashed.at[rows, lanes]
            into = pl.ds((block + 1) * BLOCK, BLOCK)
            log_share = jnp.log2(LOSS_SCALE / total[:, into])
            relative = ids[block + 1] - tile * TABLE_TILE
            return held, made.at[:, into], log_share, relative, prob[block + 1]

        lasts = [logit_grads(*of(block), FAST_SLOTS) for block in range(blocks)]
        for block in range(blocks):
            count = counts[tile * blocks + block]

            @pl.when(count > FAST_SLOTS)
            def _(block=block, count=count):
                more_targets(*of(block), lasts[block], FAST_SLOTS, count)

        @pl.when((chunks[0] > 1) & (index > 0))
        def _():
            more_lookups(before)

        ready[...] = made[...]
        return 0

    @pl.when(now)
    def _():
        left[:, 0:BLOCK] = own_columns[0]
        left[:, BLOCK : 2 * BLOCK] = side_columns[0]
        left[:, 2 * BLOCK : 3 * BLOCK] = side_columns[1]
        left[:, 3 * BLOCK : 4 * BLOCK] = far_columns[0]
        left[:, 4 * BLOCK :] = packed_cot[0]
        ready[...] = jnp.zeros_like(ready)
        lax.fori_loop(0, tiles, step, 0)
        put(tiles - 1, product())

        @pl.when(chunks[0] > 1)
        def _():
            more_lookups(tiles - 1)


def smem():
    return pl.BlockSpec(memory_space=pltpu.SMEM)


def vmem():
    return pl.BlockSpec(memory_space=pltpu.VMEM)


def whole(shape):
    return pl.BlockSpec(shape, lambda *_: (0,) * len(shape))


def shape_of(shape, dtype):
    return jax.ShapeDtypeStruct(shape, dtype)


def small_call(kernel, name, outs, *args, scratch=(), limit=4 << 20):
    return pl.pallas_call(
        kernel,
        out_shape=tuple(shape_of(shape, dtype) for shape, dtype, _ in outs),
        in_specs=[vmem()] * len(args),
        out_specs=tuple(space() for _, _, space in outs),
        scratch_shapes=scratch,
        compiler_params=pltpu.CompilerParams(vmem_limit_bytes=limit),
        name=name,
    )(*args)


def logits_call(embed, near, far, columns, fresh):
    blocks = len(near)
    rows, width = embed.shape
    tokens = blocks * BLOCK
    length = ROW_STEP if fresh else LONG_STEP
    steps = ROW_STEP * (PADDED // ROW_STEP) // length
    table = whole((PADDED, width))
    out_specs = [
        whole((PADDED, tokens)),
        whole((1, tokens)),
        whole((blocks, columns, BLOCK)),
    ]
    out_shape = [
        pltpu.VMEM((PADDED, tokens), jnp.float32),
        shape_of((1, tokens), jnp.float32),
        shape_of((blocks, columns, BLOCK), jnp.bfloat16),
    ]
    scratch = [
        pltpu.VMEM((blocks, width, BLOCK), jnp.bfloat16),
        pltpu.VMEM((8, tokens), jnp.float32),
    ]
    if fresh:
        out_specs.append(table)
        out_shape.append(pltpu.VMEM((PADDED, width), embed.dtype))
        scratch.append(pltpu.SemaphoreType.DMA((steps,)))
    return pl.pallas_call(
        functools.partial(logit_kernel, blocks, fresh),
        grid=(steps,),
        in_specs=[pl.BlockSpec(memory_space=pltpu.HBM) if fresh else table]
        + [whole((width, HALF))] * (2 * blocks),
        out_specs=out_specs,
        out_shape=out_shape,
        scratch_shapes=scratch,
        compiler_params=pltpu.CompilerParams(vmem_limit_bytes=(3 + 2 * blocks) << 20),
        cost_estimate=pl.CostEstimate(
            flops=2 * rows * width * tokens,
            bytes_accessed=rows * tokens * 4 + (2 * rows * width if fresh else 0),
            transcendentals=2 * rows * tokens,
        ),
        name=f"logits_{blocks}",
    )(pltpu.with_memory_space_constraint(embed, pltpu.HBM) if fresh else embed, *near, *far)


def index_of(x, z, y, core):
    return ((x * SIDE + z) * SIDE + y) * 2 + core


def route_by(target):
    pairs = []
    for x in range(SIDE):
        for z in range(SIDE):
            for y in range(SIDE):
                for core in range(2):
                    pairs.append((index_of(x, z, y, core), index_of(*target(x, z, y, core))))
    return pairs


def along(axis, core, by, place):
    x, z, y = place
    if axis == 2:
        x = (x + (by if core == 0 else -by)) % SIDE
    elif axis == core:
        y = (y + by) % SIDE
    else:
        z = (z + by) % SIDE
    return x, z, y, core


def fetch(value, axis, by):
    return lax.ppermute(value, EVERY, route_by(lambda x, z, y, c: along(axis, c, -by, (x, z, y))))


def hand_on(value, axis, by):
    return lax.ppermute(value, EVERY, route_by(lambda x, z, y, c: along(axis, c, by, (x, z, y))))


def exchange(value, axis, bit):
    def other(x, z, y, core):
        return along(axis, core, ((y if axis == core else z) ^ bit) - (y if axis == core else z), (x, z, y))

    return lax.ppermute(value, EVERY, route_by(other))


def swap(value):
    return lax.ppermute(value, EVERY, route_by(lambda x, z, y, c: (x, z, y, 1 - c)))


def fetch_parts(value, axis):
    return [value] + [fetch(value, axis, by) for by in OFFSETS[1:]]


def fetch_all(value, axis):
    return jnp.concatenate(fetch_parts(value, axis), axis=0)


def halves(core_zero, low, high):
    return jnp.where(core_zero, low, high), jnp.where(core_zero, high, low)


def in_core_order(core_zero, kept, got):
    return jnp.where(
        core_zero, jnp.concatenate([kept, got], 0), jnp.concatenate([got, kept], 0)
    )


def side_values(core_zero, after, token_ids, lookup_cot, teacher_ids, teacher_logits):
    here_tokens, thin = lookup_cot.shape
    share = teacher_ids.shape[0]
    pack = jnp.concatenate(
        [
            jnp.concatenate([teacher_logits, teacher_ids.astype(jnp.float32)], axis=1),
            token_ids.astype(jnp.float32).reshape(here_tokens // HALF, HALF),
            jnp.zeros((8 - here_tokens // HALF, HALF), jnp.float32),
        ],
        axis=0,
    )
    pack, turned, _ = lax.optimization_barrier((pack, lookup_cot.T, after))
    moved = lax.ppermute(
        turned,
        EVERY,
        route_by(lambda x, z, y, c: (z, x, y, c)),
    ).astype(jnp.float32)
    packs = [pack] + [
        lax.ppermute(pack, "dp", [((k + by) % SIDE, k) for k in range(SIDE)])
        for by in OFFSETS[1:]
    ]
    far_away = [packs[0], packs[1], packs[3], packs[2]]
    sides = [
        jnp.concatenate(
            [
                moved[:, half * HALF : (half + 1) * HALF],
                far_away[2 * half][:share],
                far_away[2 * half + 1][:share],
            ],
            axis=0,
        )
        for half in range(2)
    ]
    return *halves(core_zero, *sides), jnp.stack(packs)


def per_device(hidden, embed, token_ids, lookup_cot, teacher_ids, teacher_logits):
    rows, width = embed.shape
    here_tokens, thin = hidden.shape
    dp = SIDE
    vocab = 2 * SIDE * SIDE
    tokens = here_tokens * dp
    top = teacher_ids.shape[1]
    share = here_tokens // vocab
    columns = width // dp
    core_zero = lax.axis_index("core") == 0

    flat = hidden.T
    kept, given = halves(core_zero, flat[:, :HALF], flat[:, HALF:])
    pair = in_core_order(core_zero, kept, swap(given))
    row = fetch_all(pair, 0)
    own_near = fetch_all(row, 1)
    side = side_values(core_zero, row, token_ids, lookup_cot, teacher_ids, teacher_logits)
    own_near, kept, given, packs = lax.optimization_barrier((own_near, *side))
    first_near = fetch(own_near, 2, 1)
    second_near = fetch(own_near, 2, -1)
    own_far = swap(own_near)
    own_squashed, own_total, own_columns, table = logits_call(
        embed, [own_near], [own_far], columns, True
    )
    given = lax.optimization_barrier((given, own_total))[0]
    side = in_core_order(core_zero, kept, swap(given))
    first_near, second_near, side = lax.optimization_barrier((first_near, second_near, side))
    opposite_near = fetch(first_near, 2, 1)
    first_far = swap(second_near)
    second_far = swap(first_near)
    side_parts = fetch_parts(side, 0)
    side_squashed, side_total, side_columns = logits_call(
        table, [first_near, second_near], [first_far, second_far], columns, False
    )
    side_parts, opposite_near, side_total = lax.optimization_barrier(
        (side_parts, opposite_near, side_total)
    )
    opposite_far = swap(opposite_near)
    side_parts = fetch_parts(jnp.concatenate(side_parts, axis=0), 1)
    far_squashed, far_total, far_columns = logits_call(
        table, [opposite_near], [opposite_far], columns, False
    )
    side_parts, far_total = lax.optimization_barrier((side_parts, far_total))
    side_near = jnp.concatenate(side_parts, axis=0)
    side_far = swap(side_near)

    total = jnp.concatenate([own_total, side_total, far_total], axis=1)
    got = swap(total)
    total = total + jnp.concatenate(
        [
            got[:, :BLOCK],
            got[:, 2 * BLOCK : 3 * BLOCK],
            got[:, BLOCK : 2 * BLOCK],
            got[:, 3 * BLOCK :],
        ],
        axis=1,
    )
    for axis in (0, 1):
        for bit in (1, 2):
            total = total + exchange(total, axis, bit)

    cot, ids, prob, row_counts, column_counts = small_call(
        functools.partial(teacher_kernel, rows, thin),
        "teacher_prep",
        [
            ((width, BLOCK), jnp.float32, vmem),
            ((dp, top, BLOCK), jnp.int32, vmem),
            ((dp, top, BLOCK), jnp.float32, vmem),
            ((PADDED // GRAD_TILE,), jnp.int32, smem),
            ((PADDED // TABLE_TILE * (dp - 1),), jnp.int32, smem),
        ],
        side_near,
        side_far,
        scratch=[pltpu.VMEM((dp, BLOCK, 2 * top), jnp.float32)],
    )
    packed_cot, packed_ids, chunks = small_call(
        functools.partial(lookup_kernel, rows, share),
        "lookup_prep",
        [
            ((dp, columns, BLOCK), jnp.bfloat16, vmem),
            ((dp, 1, BLOCK), jnp.int32, vmem),
            ((1,), jnp.int32, smem),
        ],
        packs,
        cot,
        scratch=[pltpu.VMEM((1, tokens), jnp.float32)],
    )

    scattered = (SIDE, SIDE, thin + 8, BLOCK)
    own_grads, keep, give = pl.pallas_call(
        hidden_grad_kernel,
        in_specs=[smem()] + [vmem()] * 5,
        out_specs=[vmem()] * 3,
        out_shape=(
            pltpu.VMEM((PADDED, BLOCK), jnp.bfloat16),
            shape_of(scattered, jnp.float32),
            shape_of(scattered, jnp.float32),
        ),
        scratch_shapes=[
            pltpu.VMEM((BLOCK, width), jnp.float32),
            pltpu.VMEM((width, BLOCK), jnp.float32),
            pltpu.VMEM((8, BLOCK), jnp.float32),
            pltpu.VMEM((GRAD_TILE, BLOCK), jnp.bfloat16),
            pltpu.VMEM((GRAD_TILE, BLOCK), jnp.bfloat16),
        ],
        compiler_params=pltpu.CompilerParams(vmem_limit_bytes=10 << 20),
        cost_estimate=pl.CostEstimate(
            flops=2 * rows * width * BLOCK,
            bytes_accessed=rows * BLOCK * 6,
            transcendentals=rows * BLOCK,
        ),
        name="hidden_grads",
    )(row_counts, table, own_squashed, total, ids, prob)

    def table_grads(so_far):
        fresh = so_far is None
        started = [] if fresh else [so_far]
        operands = [
            column_counts,
            chunks,
            own_grads,
            side_squashed,
            far_squashed,
            total,
            ids,
            prob,
            packed_cot,
            packed_ids,
            own_columns,
            side_columns,
            far_columns,
        ]
        made = PADDED // 2
        half = (columns, PADDED // 2)
        return pl.pallas_call(
            functools.partial(table_grad_kernel, width, fresh),
            grid=(1 if fresh else 2,),
            in_specs=[smem()] * 2
            + [whole(operand.shape) for operand in operands[2:]]
            + [whole(half) for _ in started],
            out_specs=pl.BlockSpec(half, lambda n: (0, n)),
            out_shape=pltpu.VMEM(half, jnp.bfloat16)
            if fresh
            else shape_of((columns, rows), jnp.bfloat16),
            scratch_shapes=[
                pltpu.VMEM((columns, (dp + 1) * BLOCK), jnp.bfloat16),
                pltpu.VMEM((TABLE_TILE, (dp + 1) * BLOCK), jnp.bfloat16),
                pltpu.VMEM((TABLE_TILE, (dp + 1) * BLOCK), jnp.bfloat16),
            ],
            compiler_params=pltpu.CompilerParams(vmem_limit_bytes=12 << 20),
            cost_estimate=pl.CostEstimate(
                flops=2 * made * columns * (tokens + BLOCK),
                bytes_accessed=rows * columns * 2,
                transcendentals=made * tokens,
            ),
            name="table_grads_start" if fresh else "table_grads_rest",
        )(*operands, *started)

    quarter = (SIDE, thin + 8, BLOCK)
    got, packed_cot, packed_ids = lax.optimization_barrier((swap(give), packed_cot, packed_ids))
    parts = small_call(halve_kernel, "halve", [(quarter, jnp.float32, vmem)] * SIDE, keep, got)
    travelling = [hand_on(part, 1, by) for part, by in zip(parts[1:], OFFSETS[1:])]
    embed_grad = table_grads(None)
    travelling, embed_grad = lax.optimization_barrier((travelling, embed_grad))
    parts = small_call(
        quarter_kernel,
        "quarter",
        [(quarter[1:], jnp.float32, vmem)] * SIDE,
        parts[0],
        *travelling,
    )
    travelling = [hand_on(part, 0, by) for part, by in zip(parts[1:], OFFSETS[1:])]
    embed_grad = table_grads(embed_grad)
    parts = [parts[0]] + travelling

    hidden_grad, divergence = small_call(
        finish_kernel,
        "finish",
        [((thin, BLOCK), jnp.bfloat16, vmem), ((1, HALF), jnp.float32, vmem)],
        total,
        teacher_logits,
        *parts,
    )
    return (hidden_grad.T, embed_grad.T, divergence[0, :share])


def solution(mesh):
    dp, vocab = (mesh.shape[name] for name in ("dp", "vocab"))
    fine = Mesh(mesh.devices.reshape(dp, SIDE, SIDE, vocab // (SIDE * SIDE)), EVERY)
    return jax.shard_map(
        per_device,
        mesh=fine,
        in_specs=(
            P("dp", RING),
            P(RING, None),
            P("dp"),
            P("dp", RING),
            P(EVERY, None),
            P(EVERY, None),
        ),
        out_specs=(P("dp", RING), P(RING, "dp"), P(EVERY)),
        check_vma=False,
    )
```

profile of v0, /device:TPU:0, one launch (start us, length us, event | category | flops | bytes accessed | tf_op | source)
XLA Modules:
  0.0 157.3 jit_solution(15029934834186239498)
XLA Ops:
  3.0 3.2 %collective-permute-start.1 = (bf16[144,128]{1,0:T(8,128)(2,1)S(1)}, bf16[144,128]{1,0:T(8,128)(2,1)S(1)}, u32[]{:S(2)}, u32[]{:S(2)}) collective-permute-start(bf16[144,128]{1,0:T(8,128)(2,1)S(1)} %get-tuple-element.122), channel_id=1, source_target_pairs={{0,6},{1,25},{2,0},{3,27},{4,2},{5,29},{6,4},{7,31},{8,14},{9,1},{... | collective-permute-start | bytes 110600 | tf_op jit(solution)/shard_map/ppermute | solution.py:572
  6.1 2.2 %collective-permute-start.3 = (bf16[144,128]{1,0:T(8,128)(2,1)S(1)}, bf16[144,128]{1,0:T(8,128)(2,1)S(1)}, u32[]{:S(2)}, u32[]{:S(2)}) collective-permute-start(bf16[144,128]{1,0:T(8,128)(2,1)S(1)} %get-tuple-element.122), channel_id=1, source_target_pairs={{0,4},{1,17},{2,6},{3,19},{4,0},{5,21},{6,2},{7,23},{8,12},{9,25},... | collective-permute-start | bytes 110600 | tf_op jit(solution)/shard_map/ppermute | solution.py:572
  9.1 2.2 %collective-permute-done.2 = bf16[144,128]{1,0:T(8,128)(2,1)S(1)} collective-permute-done((bf16[144,128]{1,0:T(8,128)(2,1)S(1)}, bf16[144,128]{1,0:T(8,128)(2,1)S(1)}, u32[]{:S(2)}, u32[]{:S(2)}) %collective-permute-start.2) | collective-permute-done | bytes 36896 | tf_op jit(solution)/shard_map/ppermute | solution.py:572
  11.7 2.8 %collective-permute-start.8 = (f32[16,128]{1,0:T(8,128)S(1)}, f32[16,128]{1,0:T(8,128)S(1)}, u32[]{:S(2)}, u32[]{:S(2)}) collective-permute-start(f32[16,128]{1,0:T(8,128)S(1)} %maximum_maximum_fusion), channel_id=1, source_target_pairs={{32,0},{64,32},{96,64},{0,96},{33,1},{65,33},{97,65},{1,97},{34,2}... | collective-permute-start | bytes 24584 | tf_op jit(solution)/shard_map/ppermute | solution.py:626
  14.5 2.3 %collective-permute-start.9 = (f32[16,128]{1,0:T(8,128)S(1)}, f32[16,128]{1,0:T(8,128)S(1)}, u32[]{:S(2)}, u32[]{:S(2)}) collective-permute-start(f32[16,128]{1,0:T(8,128)S(1)} %maximum_maximum_fusion), channel_id=1, source_target_pairs={{64,0},{96,32},{0,64},{32,96},{65,1},{97,33},{1,65},{33,97},{66,2}... | collective-permute-start | bytes 24584 | tf_op jit(solution)/shard_map/ppermute | solution.py:626
  16.8 4.0 %collective-permute-start.4 = (bf16[576,128]{1,0:T(8,128)(2,1)S(1)}, bf16[576,128]{1,0:T(8,128)(2,1)S(1)}, u32[]{:S(2)}, u32[]{:S(2)}) collective-permute-start(bf16[576,128]{1,0:T(8,128)(2,1)S(1)} %pad_maximum_fusion), channel_id=1, source_target_pairs={{0,24},{1,7},{2,26},{3,1},{4,28},{5,3},{6,30},{7,5},{8,0},{9,15},{... | collective-permute-start | bytes 442376 | tf_op jit(solution)/shard_map/ppermute | solution.py:572
  20.9 1.9 %collective-permute-start.6 = (bf16[576,128]{1,0:T(8,128)(2,1)S(1)}, bf16[576,128]{1,0:T(8,128)(2,1)S(1)}, u32[]{:S(2)}, u32[]{:S(2)}) collective-permute-start(bf16[576,128]{1,0:T(8,128)(2,1)S(1)} %pad_maximum_fusion), channel_id=1, source_target_pairs={{0,16},{1,5},{2,18},{3,7},{4,20},{5,1},{6,22},{7,3},{8,24},{9,13},... | collective-permute-start | bytes 442376 | tf_op jit(solution)/shard_map/ppermute | solution.py:572
  24.4 4.4 %collective-permute-done.5 = bf16[576,128]{1,0:T(8,128)(2,1)S(1)} collective-permute-done((bf16[576,128]{1,0:T(8,128)(2,1)S(1)}, bf16[576,128]{1,0:T(8,128)(2,1)S(1)}, u32[]{:S(2)}, u32[]{:S(2)}) %collective-permute-start.5) | collective-permute-done | bytes 147488 | tf_op jit(solution)/shard_map/ppermute | solution.py:572
  29.0 4.7 %collective-permute-start.12 = (bf16[2304,128]{1,0:T(8,128)(2,1)S(1)}, bf16[2304,128]{1,0:T(8,128)(2,1)S(1)}, u32[]{:S(2)}, u32[]{:S(2)}) collective-permute-start(bf16[2304,128]{1,0:T(8,128)(2,1)S(1)} %constant_dynamic-update-slice_fusion.refs_0_), channel_id=1, source_target_pairs={{0,96},{1,33},{2,98},{3,35},{4,100},{5,37},{6,102},{7,39},{8,104},... | collective-permute-start | bytes 1769480 | tf_op jit(solution)/shard_map/ppermute | solution.py:572
  33.7 8.5 %logits_1.2 = (f32[4096,256]{1,0:T(8,128)S(1)}, f32[1,256]{1,0:T(1,128)S(1)}, bf16[1,576,256]{2,1,0:T(8,128)(2,1)S(1)}, bf16[4096,2304]{1,0:T(8,128)(2,1)S(1)}) custom-call(bf16[4000,2304]{1,0:T(8,128)(2,1)} %embed.1, bf16[2304,128]{1,0:T(8,128)(2,1)S(1)} %constant_dynamic-update-slice_fusion.refs_0_, bf16[2304,128]{1,0:T(8,128)(2,1)S(1)} %collective-permute-done.11.refs_1_), custom_call_target="tpu_custom_call" | custom-call | flops 4718592000 | bytes 22528000 | tf_op jit(solution)/shard_map/logits_1/pallas_call | solution.py:528
  43.5 3.4 %collective-permute-done.12.refs_0_ = bf16[2304,128]{1,0:T(8,128)(2,1)S(1)} collective-permute-done((bf16[2304,128]{1,0:T(8,128)(2,1)S(1)}, bf16[2304,128]{1,0:T(8,128)(2,1)S(1)}, u32[]{:S(2)}, u32[]{:S(2)}) %collective-permute-start.12) | collective-permute-done | bytes 589856 | tf_op jit(solution)/shard_map/ppermute | solution.py:572
  48.1 3.0 %collective-permute-start.18 = (bf16[2304,128]{1,0:T(8,128)(2,1)S(1)}, bf16[2304,128]{1,0:T(8,128)(2,1)S(1)}, u32[]{:S(2)}, u32[]{:S(2)}) collective-permute-start(bf16[2304,128]{1,0:T(8,128)(2,1)S(1)} %collective-permute-done.12.refs_0_), channel_id=1, source_target_pairs={{0,96},{1,33},{2,98},{3,35},{4,100},{5,37},{6,102},{7,39},{8,104},... | collective-permute-start | bytes 1769480 | tf_op jit(solution)/shard_map/ppermute | solution.py:572
  51.1 3.1 %collective-permute-start.15 = (f32[176,128]{1,0:T(8,128)S(1)}, f32[176,128]{1,0:T(8,128)S(1)}, u32[]{:S(2)}, u32[]{:S(2)}) collective-permute-start(f32[176,128]{1,0:T(8,128)S(1)} %maximum_select_fusion), channel_id=1, source_target_pairs={{0,6},{1,25},{2,0},{3,27},{4,2},{5,29},{6,4},{7,31},{8,14},{9,1},{... | collective-permute-start | bytes 270344 | tf_op jit(solution)/shard_map/ppermute | solution.py:572
  55.7 11.3 %logits_2.1 = (f32[4096,512]{1,0:T(8,128)S(1)}, f32[1,512]{1,0:T(1,128)S(1)}, bf16[2,576,256]{2,1,0:T(8,128)(2,1)S(1)}) custom-call(bf16[4096,2304]{1,0:T(8,128)(2,1)S(1)} %get-tuple-element.71.embed, bf16[2304,128]{1,0:T(8,128)(2,1)S(1)} %collective-permute-done.12.refs_0_, bf16[2304,128]{1,0:T(8,128)(2,1)S(1)} %collective-permute-done.13.refs_1_, ...), custom_call_target="tpu_custom_call" | custom-call | flops 9663676416 | bytes 8388608 | tf_op jit(solution)/shard_map/logits_2/pallas_call | solution.py:528
  67.5 2.7 %collective-permute-start.22 = (f32[704,128]{1,0:T(8,128)S(1)}, f32[704,128]{1,0:T(8,128)S(1)}, u32[]{:S(2)}, u32[]{:S(2)}) collective-permute-start(f32[704,128]{1,0:T(8,128)S(1)} %constant_dynamic-update-slice_fusion.7), channel_id=1, source_target_pairs={{0,8},{1,3},{2,10},{3,5},{4,12},{5,7},{6,14},{7,1},{8,16},{9,11},{... | collective-permute-start | bytes 1081352 | tf_op jit(solution)/shard_map/ppermute | solution.py:572
  70.2 2.0 %collective-permute-start.23 = (f32[704,128]{1,0:T(8,128)S(1)}, f32[704,128]{1,0:T(8,128)S(1)}, u32[]{:S(2)}, u32[]{:S(2)}) collective-permute-start(f32[704,128]{1,0:T(8,128)S(1)} %constant_dynamic-update-slice_fusion.7), channel_id=1, source_target_pairs={{0,16},{1,5},{2,18},{3,7},{4,20},{5,1},{6,22},{7,3},{8,24},{9,13},... | collective-permute-start | bytes 1081352 | tf_op jit(solution)/shard_map/ppermute | solution.py:572
  72.2 5.9 %logits_1.3 = (f32[4096,256]{1,0:T(8,128)S(1)}, f32[1,256]{1,0:T(1,128)S(1)}, bf16[1,576,256]{2,1,0:T(8,128)(2,1)S(1)}) custom-call(bf16[4096,2304]{1,0:T(8,128)(2,1)S(1)} %get-tuple-element.71.embed, bf16[2304,128]{1,0:T(8,128)(2,1)S(1)} %collective-permute-done.18.refs_0_, bf16[2304,128]{1,0:T(8,128)(2,1)S(1)} %collective-permute-done.24.refs_1_), custom_call_target="tpu_custom_call" | custom-call | flops 4831838208 | bytes 4194304 | tf_op jit(solution)/shard_map/logits_1/pallas_call | solution.py:528
  78.1 3.3 %collective-permute-done.23 = f32[704,128]{1,0:T(8,128)S(1)} collective-permute-done((f32[704,128]{1,0:T(8,128)S(1)}, f32[704,128]{1,0:T(8,128)S(1)}, u32[]{:S(2)}, u32[]{:S(2)}) %collective-permute-start.23) | collective-permute-done | bytes 360480 | tf_op jit(solution)/shard_map/ppermute | solution.py:572
  82.3 2.6 %collective-permute-done.25 = f32[1,1024]{1,0:T(1,128)S(1)} collective-permute-done((f32[1,1024]{1,0:T(1,128)S(1)}, f32[1,1024]{1,0:T(1,128)S(1)}, u32[]{:S(2)}, u32[]{:S(2)}) %collective-permute-start.25) | collective-permute-done | bytes 4128 | tf_op jit(solution)/shard_map/ppermute | solution.py:587
  84.9 2.7 %collective-permute-start.26 = (f32[1,1024]{1,0:T(1,128)S(1)}, f32[1,1024]{1,0:T(1,128)S(1)}, u32[]{:S(2)}, u32[]{:S(2)}) collective-permute-start(f32[1,1024]{1,0:T(1,128)S(1)} %maximum_add_fusion), channel_id=1, source_target_pairs={{0,2},{1,9},{2,0},{3,11},{4,6},{5,13},{6,4},{7,15},{8,10},{9,1},{1... | collective-permute-start | bytes 12296 | tf_op jit(solution)/shard_map/ppermute | solution.py:583
  87.6 1.6 %collective-permute-done.26 = f32[1,1024]{1,0:T(1,128)S(1)} collective-permute-done((f32[1,1024]{1,0:T(1,128)S(1)}, f32[1,1024]{1,0:T(1,128)S(1)}, u32[]{:S(2)}, u32[]{:S(2)}) %collective-permute-start.26) | collective-permute-done | bytes 4128 | tf_op jit(solution)/shard_map/ppermute | solution.py:583
  90.7 3.7 %collective-permute-done.27 = f32[1,1024]{1,0:T(1,128)S(1)} collective-permute-done((f32[1,1024]{1,0:T(1,128)S(1)}, f32[1,1024]{1,0:T(1,128)S(1)}, u32[]{:S(2)}, u32[]{:S(2)}) %collective-permute-start.27) | collective-permute-done | bytes 4128 | tf_op jit(solution)/shard_map/ppermute | solution.py:583
  95.4 2.6 %collective-permute-done.28 = f32[1,1024]{1,0:T(1,128)S(1)} collective-permute-done((f32[1,1024]{1,0:T(1,128)S(1)}, f32[1,1024]{1,0:T(1,128)S(1)}, u32[]{:S(2)}, u32[]{:S(2)}) %collective-permute-start.28) | collective-permute-done | bytes 4128 | tf_op jit(solution)/shard_map/ppermute | solution.py:583
  97.9 2.0 %collective-permute-start.29 = (f32[1,1024]{1,0:T(1,128)S(1)}, f32[1,1024]{1,0:T(1,128)S(1)}, u32[]{:S(2)}, u32[]{:S(2)}) collective-permute-start(f32[1,1024]{1,0:T(1,128)S(1)} %add.26), channel_id=1, source_target_pairs={{0,16},{1,5},{2,18},{3,7},{4,20},{5,1},{6,22},{7,3},{8,24},{9,13},... | collective-permute-start | bytes 12296 | tf_op jit(solution)/shard_map/ppermute | solution.py:583
  100.0 3.1 %collective-permute-done.29 = f32[1,1024]{1,0:T(1,128)S(1)} collective-permute-done((f32[1,1024]{1,0:T(1,128)S(1)}, f32[1,1024]{1,0:T(1,128)S(1)}, u32[]{:S(2)}, u32[]{:S(2)}) %collective-permute-start.29) | collective-permute-done | bytes 4128 | tf_op jit(solution)/shard_map/ppermute | solution.py:583
  103.1 2.2 %teacher_prep.1 = (f32[2304,256]{1,0:T(8,128)S(1)}, s32[4,64,256]{2,1,0:T(8,128)S(1)}, f32[4,64,256]{2,1,0:T(8,128)S(1)}, s32[8]{0:T(128)S(1)}, s32[48]{0:T(128)S(1)}) custom-call(f32[2816,128]{1,0:T(8,128)S(1)} %constant_dynamic-update-slice_fusion.14.near, f32[2816,128]{1,0:T(8,128)S(1)} %collective-permute-done.30.far), custom_call_target="tpu_custom_call" | custom-call | tf_op jit(solution)/shard_map/teacher_prep/pallas_call | solution.py:492
  105.2 11.9 %hidden_grads.1 = (bf16[4096,256]{1,0:T(8,128)(2,1)S(1)}, f32[4,4,80,256]{3,2,1,0:T(8,128)S(1)}, f32[4,4,80,256]{3,2,1,0:T(8,128)S(1)}) custom-call(s32[8]{0:T(128)S(1)} %get-tuple-element.86.counts, bf16[4096,2304]{1,0:T(8,128)(2,1)S(1)} %get-tuple-element.71.embed, f32[4096,256]{1,0:T(8,128)S(1)} %get-tuple-element.87.squashed, f32[1,1024]{1,0:T(1,128)S(1)} %add.27.total, ...), custom_call_target="tpu_custom_call" | custom-call | flops 4718592000 | bytes 6144000 | tf_op jit(solution)/shard_map/hidden_grads/pallas_call | solution.py:733
  117.2 1.8 %lookup_prep.1 = (bf16[4,576,256]{2,1,0:T(8,128)(2,1)S(1)}, s32[4,1,256]{2,1,0:T(1,128)S(1)}, s32[1]{0:T(128)}) custom-call(f32[4,16,128]{2,1,0:T(8,128)S(1)} %pad_maximum_fusion.3.packs, f32[2304,256]{1,0:T(8,128)S(1)} %get-tuple-element.93.cot), custom_call_target="tpu_custom_call" | custom-call | tf_op jit(solution)/shard_map/lookup_prep/pallas_call | solution.py:492
  121.5 2.2 %collective-permute-start.33 = (f32[4,80,256]{2,1,0:T(8,128)S(1)}, f32[4,80,256]{2,1,0:T(8,128)S(1)}, u32[]{:S(2)}, u32[]{:S(2)}) collective-permute-start(f32[4,80,256]{2,1,0:T(8,128)S(1)} %get-tuple-element.99), channel_id=1, source_target_pairs={{0,24},{1,7},{2,26},{3,1},{4,28},{5,3},{6,30},{7,5},{8,0},{9,15},{... | collective-permute-start | bytes 983048 | tf_op jit(solution)/shard_map/ppermute | solution.py:576
  124.6 12.7 %table_grads_start.1.refs_0_ = bf16[576,2048]{1,0:T(8,128)(2,1)S(1)} custom-call(s32[48]{0:T(128)S(1)} %get-tuple-element.101.counts, s32[1]{0:T(128)} %get-tuple-element.102.chunks, bf16[4096,256]{1,0:T(8,128)(2,1)S(1)} %get-tuple-element.103.own_grads, f32[4096,512]{1,0:T(8,128)S(1)} %get-tuple-element.104.side_squashed, ...), custom_call_target="tpu_custom_call" | custom-call | flops 3019898880 | bytes 4608000 | tf_op jit(solution)/shard_map/table_grads_start/pallas_call | solution.py:778
  137.4 2.1 %collective-permute-start.35 = (f32[80,256]{1,0:T(8,128)S(1)}, f32[80,256]{1,0:T(8,128)S(1)}, u32[]{:S(2)}, u32[]{:S(2)}) collective-permute-start(f32[80,256]{1,0:T(8,128)S(1)} %get-tuple-element.115), channel_id=1, source_target_pairs={{0,2},{1,9},{2,4},{3,11},{4,6},{5,13},{6,0},{7,15},{8,10},{9,17},{... | collective-permute-start | bytes 245768 | tf_op jit(solution)/shard_map/ppermute | solution.py:576
  141.7 14.4 %table_grads_rest.1 = bf16[576,4000]{1,0:T(8,128)(2,1)} custom-call(s32[48]{0:T(128)S(1)} %get-tuple-element.101.counts, s32[1]{0:T(128)} %get-tuple-element.102.chunks, bf16[4096,256]{1,0:T(8,128)(2,1)S(1)} %get-tuple-element.103.own_grads, f32[4096,512]{1,0:T(8,128)S(1)} %get-tuple-element.104.side_squashed, ...), custom_call_target="tpu_custom_call" | custom-call | flops 3019898880 | bytes 4608000 | tf_op jit(solution)/shard_map/table_grads_rest/pallas_call | solution.py:778
  (97 shorter events, 19.9 us)
Async XLA Ops:
  3.0 6.1 %collective-permute-start.1 = (bf16[144,128]{1,0:T(8,128)(2,1)S(1)}, bf16[144,128]{1,0:T(8,128)(2,1)S(1)}, u32[]{:S(2)}, u32[]{:S(2)}) collective-permute-start(bf16[144,128]{1,0:T(8,128)(2,1)S(1)} %get-tuple-element.122), channel_id=1, source_target_pairs={{0,6},{1,25},{2,0},{3,27},{4,2},{5,29},{6,4},{7,31},{8,14},{9,1},{... | collective-permute-start | bytes 110600 | tf_op jit(solution)/shard_map/ppermute | solution.py:572
  6.1 5.2 %collective-permute-start.2 = (bf16[144,128]{1,0:T(8,128)(2,1)S(1)}, bf16[144,128]{1,0:T(8,128)(2,1)S(1)}, u32[]{:S(2)}, u32[]{:S(2)}) collective-permute-start(bf16[144,128]{1,0:T(8,128)(2,1)S(1)} %get-tuple-element.122), channel_id=1, source_target_pairs={{0,2},{1,9},{2,4},{3,11},{4,6},{5,13},{6,0},{7,15},{8,10},{9,17},{... | collective-permute-start | bytes 110600 | tf_op jit(solution)/shard_map/ppermute | solution.py:572
  6.1 5.6 %collective-permute-start.3 = (bf16[144,128]{1,0:T(8,128)(2,1)S(1)}, bf16[144,128]{1,0:T(8,128)(2,1)S(1)}, u32[]{:S(2)}, u32[]{:S(2)}) collective-permute-start(bf16[144,128]{1,0:T(8,128)(2,1)S(1)} %get-tuple-element.122), channel_id=1, source_target_pairs={{0,4},{1,17},{2,6},{3,19},{4,0},{5,21},{6,2},{7,23},{8,12},{9,25},... | collective-permute-start | bytes 110600 | tf_op jit(solution)/shard_map/ppermute | solution.py:572
  11.7 9.2 %collective-permute-start.8 = (f32[16,128]{1,0:T(8,128)S(1)}, f32[16,128]{1,0:T(8,128)S(1)}, u32[]{:S(2)}, u32[]{:S(2)}) collective-permute-start(f32[16,128]{1,0:T(8,128)S(1)} %maximum_maximum_fusion), channel_id=1, source_target_pairs={{32,0},{64,32},{96,64},{0,96},{33,1},{65,33},{97,65},{1,97},{34,2}... | collective-permute-start | bytes 24584 | tf_op jit(solution)/shard_map/ppermute | solution.py:626
  14.5 8.3 %collective-permute-start.10 = (f32[16,128]{1,0:T(8,128)S(1)}, f32[16,128]{1,0:T(8,128)S(1)}, u32[]{:S(2)}, u32[]{:S(2)}) collective-permute-start(f32[16,128]{1,0:T(8,128)S(1)} %maximum_maximum_fusion), channel_id=1, source_target_pairs={{96,0},{0,32},{32,64},{64,96},{97,1},{1,33},{33,65},{65,97},{98,2}... | collective-permute-start | bytes 24584 | tf_op jit(solution)/shard_map/ppermute | solution.py:626
  14.5 9.7 %collective-permute-start.9 = (f32[16,128]{1,0:T(8,128)S(1)}, f32[16,128]{1,0:T(8,128)S(1)}, u32[]{:S(2)}, u32[]{:S(2)}) collective-permute-start(f32[16,128]{1,0:T(8,128)S(1)} %maximum_maximum_fusion), channel_id=1, source_target_pairs={{64,0},{96,32},{0,64},{32,96},{65,1},{97,33},{1,65},{33,97},{66,2}... | collective-permute-start | bytes 24584 | tf_op jit(solution)/shard_map/ppermute | solution.py:626
  16.8 7.5 %collective-permute-start.4 = (bf16[576,128]{1,0:T(8,128)(2,1)S(1)}, bf16[576,128]{1,0:T(8,128)(2,1)S(1)}, u32[]{:S(2)}, u32[]{:S(2)}) collective-permute-start(bf16[576,128]{1,0:T(8,128)(2,1)S(1)} %pad_maximum_fusion), channel_id=1, source_target_pairs={{0,24},{1,7},{2,26},{3,1},{4,28},{5,3},{6,30},{7,5},{8,0},{9,15},{... | collective-permute-start | bytes 442376 | tf_op jit(solution)/shard_map/ppermute | solution.py:572
  20.9 7.9 %collective-permute-start.5 = (bf16[576,128]{1,0:T(8,128)(2,1)S(1)}, bf16[576,128]{1,0:T(8,128)(2,1)S(1)}, u32[]{:S(2)}, u32[]{:S(2)}) collective-permute-start(bf16[576,128]{1,0:T(8,128)(2,1)S(1)} %pad_maximum_fusion), channel_id=1, source_target_pairs={{0,8},{1,3},{2,10},{3,5},{4,12},{5,7},{6,14},{7,1},{8,16},{9,11},{... | collective-permute-start | bytes 442376 | tf_op jit(solution)/shard_map/ppermute | solution.py:572
  20.9 7.9 %collective-permute-start.6 = (bf16[576,128]{1,0:T(8,128)(2,1)S(1)}, bf16[576,128]{1,0:T(8,128)(2,1)S(1)}, u32[]{:S(2)}, u32[]{:S(2)}) collective-permute-start(bf16[576,128]{1,0:T(8,128)(2,1)S(1)} %pad_maximum_fusion), channel_id=1, source_target_pairs={{0,16},{1,5},{2,18},{3,7},{4,20},{5,1},{6,22},{7,3},{8,24},{9,13},... | collective-permute-start | bytes 442376 | tf_op jit(solution)/shard_map/ppermute | solution.py:572
  28.9 4.8 %collective-permute-start.11 = (bf16[2304,128]{1,0:T(8,128)(2,1)S(1)}, bf16[2304,128]{1,0:T(8,128)(2,1)S(1)}, u32[]{:S(2)}, u32[]{:S(2)}) collective-permute-start(bf16[2304,128]{1,0:T(8,128)(2,1)S(1)} %constant_dynamic-update-slice_fusion.refs_0_), channel_id=1, source_target_pairs={{0,1},{1,0},{2,3},{3,2},{4,5},{5,4},{6,7},{7,6},{8,9},{9,8},{10,11... | collective-permute-start | bytes 1769480 | tf_op jit(solution)/shard_map/ppermute | solution.py:587
  29.0 17.9 %collective-permute-start.12 = (bf16[2304,128]{1,0:T(8,128)(2,1)S(1)}, bf16[2304,128]{1,0:T(8,128)(2,1)S(1)}, u32[]{:S(2)}, u32[]{:S(2)}) collective-permute-start(bf16[2304,128]{1,0:T(8,128)(2,1)S(1)} %constant_dynamic-update-slice_fusion.refs_0_), channel_id=1, source_target_pairs={{0,96},{1,33},{2,98},{3,35},{4,100},{5,37},{6,102},{7,39},{8,104},... | collective-permute-start | bytes 1769480 | tf_op jit(solution)/shard_map/ppermute | solution.py:572
  33.7 13.9 %collective-permute-start.13 = (bf16[2304,128]{1,0:T(8,128)(2,1)S(1)}, bf16[2304,128]{1,0:T(8,128)(2,1)S(1)}, u32[]{:S(2)}, u32[]{:S(2)}) collective-permute-start(bf16[2304,128]{1,0:T(8,128)(2,1)S(1)} %constant_dynamic-update-slice_fusion.refs_0_), channel_id=1, source_target_pairs={{0,32},{1,97},{2,34},{3,99},{4,36},{5,101},{6,38},{7,103},{8,40},{... | collective-permute-start | bytes 1769480 | tf_op jit(solution)/shard_map/ppermute | solution.py:572
  47.6 6.6 %collective-permute-start.19 = (bf16[2304,128]{1,0:T(8,128)(2,1)S(1)}, bf16[2304,128]{1,0:T(8,128)(2,1)S(1)}, u32[]{:S(2)}, u32[]{:S(2)}) collective-permute-start(bf16[2304,128]{1,0:T(8,128)(2,1)S(1)} %collective-permute-done.13.refs_1_), channel_id=1, source_target_pairs={{0,1},{1,0},{2,3},{3,2},{4,5},{5,4},{6,7},{7,6},{8,9},{9,8},{10,11... | collective-permute-start | bytes 1769480 | tf_op jit(solution)/shard_map/ppermute | solution.py:587
  47.6 8.1 %collective-permute-start.20 = (bf16[2304,128]{1,0:T(8,128)(2,1)S(1)}, bf16[2304,128]{1,0:T(8,128)(2,1)S(1)}, u32[]{:S(2)}, u32[]{:S(2)}) collective-permute-start(bf16[2304,128]{1,0:T(8,128)(2,1)S(1)} %collective-permute-done.12.refs_0_), channel_id=1, source_target_pairs={{0,1},{1,0},{2,3},{3,2},{4,5},{5,4},{6,7},{7,6},{8,9},{9,8},{10,11... | collective-permute-start | bytes 1769480 | tf_op jit(solution)/shard_map/ppermute | solution.py:587
  48.1 19.0 %collective-permute-start.18 = (bf16[2304,128]{1,0:T(8,128)(2,1)S(1)}, bf16[2304,128]{1,0:T(8,128)(2,1)S(1)}, u32[]{:S(2)}, u32[]{:S(2)}) collective-permute-start(bf16[2304,128]{1,0:T(8,128)(2,1)S(1)} %collective-permute-done.12.refs_0_), channel_id=1, source_target_pairs={{0,96},{1,33},{2,98},{3,35},{4,100},{5,37},{6,102},{7,39},{8,104},... | collective-permute-start | bytes 1769480 | tf_op jit(solution)/shard_map/ppermute | solution.py:572
  51.1 15.9 %collective-permute-start.15 = (f32[176,128]{1,0:T(8,128)S(1)}, f32[176,128]{1,0:T(8,128)S(1)}, u32[]{:S(2)}, u32[]{:S(2)}) collective-permute-start(f32[176,128]{1,0:T(8,128)S(1)} %maximum_select_fusion), channel_id=1, source_target_pairs={{0,6},{1,25},{2,0},{3,27},{4,2},{5,29},{6,4},{7,31},{8,14},{9,1},{... | collective-permute-start | bytes 270344 | tf_op jit(solution)/shard_map/ppermute | solution.py:572
  54.2 12.8 %collective-permute-start.16 = (f32[176,128]{1,0:T(8,128)S(1)}, f32[176,128]{1,0:T(8,128)S(1)}, u32[]{:S(2)}, u32[]{:S(2)}) collective-permute-start(f32[176,128]{1,0:T(8,128)S(1)} %maximum_select_fusion), channel_id=1, source_target_pairs={{0,2},{1,9},{2,4},{3,11},{4,6},{5,13},{6,0},{7,15},{8,10},{9,17},{... | collective-permute-start | bytes 270344 | tf_op jit(solution)/shard_map/ppermute | solution.py:572
  54.2 12.8 %collective-permute-start.17 = (f32[176,128]{1,0:T(8,128)S(1)}, f32[176,128]{1,0:T(8,128)S(1)}, u32[]{:S(2)}, u32[]{:S(2)}) collective-permute-start(f32[176,128]{1,0:T(8,128)S(1)} %maximum_select_fusion), channel_id=1, source_target_pairs={{0,4},{1,17},{2,6},{3,19},{4,0},{5,21},{6,2},{7,23},{8,12},{9,25},... | collective-permute-start | bytes 270344 | tf_op jit(solution)/shard_map/ppermute | solution.py:572
  67.1 5.1 %collective-permute-start.24 = (bf16[2304,128]{1,0:T(8,128)(2,1)S(1)}, bf16[2304,128]{1,0:T(8,128)(2,1)S(1)}, u32[]{:S(2)}, u32[]{:S(2)}) collective-permute-start(bf16[2304,128]{1,0:T(8,128)(2,1)S(1)} %collective-permute-done.18.refs_0_), channel_id=1, source_target_pairs={{0,1},{1,0},{2,3},{3,2},{4,5},{5,4},{6,7},{7,6},{8,9},{9,8},{10,11... | collective-permute-start | bytes 1769480 | tf_op jit(solution)/shard_map/ppermute | solution.py:587
  67.2 10.9 %collective-permute-start.21 = (f32[704,128]{1,0:T(8,128)S(1)}, f32[704,128]{1,0:T(8,128)S(1)}, u32[]{:S(2)}, u32[]{:S(2)}) collective-permute-start(f32[704,128]{1,0:T(8,128)S(1)} %constant_dynamic-update-slice_fusion.7), channel_id=1, source_target_pairs={{0,24},{1,7},{2,26},{3,1},{4,28},{5,3},{6,30},{7,5},{8,0},{9,15},{... | collective-permute-start | bytes 1081352 | tf_op jit(solution)/shard_map/ppermute | solution.py:572
  67.5 10.6 %collective-permute-start.22 = (f32[704,128]{1,0:T(8,128)S(1)}, f32[704,128]{1,0:T(8,128)S(1)}, u32[]{:S(2)}, u32[]{:S(2)}) collective-permute-start(f32[704,128]{1,0:T(8,128)S(1)} %constant_dynamic-update-slice_fusion.7), channel_id=1, source_target_pairs={{0,8},{1,3},{2,10},{3,5},{4,12},{5,7},{6,14},{7,1},{8,16},{9,11},{... | collective-permute-start | bytes 1081352 | tf_op jit(solution)/shard_map/ppermute | solution.py:572
  70.2 11.2 %collective-permute-start.23 = (f32[704,128]{1,0:T(8,128)S(1)}, f32[704,128]{1,0:T(8,128)S(1)}, u32[]{:S(2)}, u32[]{:S(2)}) collective-permute-start(f32[704,128]{1,0:T(8,128)S(1)} %constant_dynamic-update-slice_fusion.7), channel_id=1, source_target_pairs={{0,16},{1,5},{2,18},{3,7},{4,20},{5,1},{6,22},{7,3},{8,24},{9,13},... | collective-permute-start | bytes 1081352 | tf_op jit(solution)/shard_map/ppermute | solution.py:572
  81.6 21.5 %collective-permute-start.30 = (f32[2816,128]{1,0:T(8,128)S(1)}, f32[2816,128]{1,0:T(8,128)S(1)}, u32[]{:S(2)}, u32[]{:S(2)}) collective-permute-start(f32[2816,128]{1,0:T(8,128)S(1)} %constant_dynamic-update-slice_fusion.14.near), channel_id=1, source_target_pairs={{0,1},{1,0},{2,3},{3,2},{4,5},{5,4},{6,7},{7,6},{8,9},{9,8},{10,11... | collective-permute-start | bytes 4325384 | tf_op jit(solution)/shard_map/ppermute | solution.py:587
  84.9 4.3 %collective-permute-start.26 = (f32[1,1024]{1,0:T(1,128)S(1)}, f32[1,1024]{1,0:T(1,128)S(1)}, u32[]{:S(2)}, u32[]{:S(2)}) collective-permute-start(f32[1,1024]{1,0:T(1,128)S(1)} %maximum_add_fusion), channel_id=1, source_target_pairs={{0,2},{1,9},{2,0},{3,11},{4,6},{5,13},{6,4},{7,15},{8,10},{9,1},{1... | collective-permute-start | bytes 12296 | tf_op jit(solution)/shard_map/ppermute | solution.py:583
  89.2 5.1 %collective-permute-start.27 = (f32[1,1024]{1,0:T(1,128)S(1)}, f32[1,1024]{1,0:T(1,128)S(1)}, u32[]{:S(2)}, u32[]{:S(2)}) collective-permute-start(f32[1,1024]{1,0:T(1,128)S(1)} %add.24), channel_id=1, source_target_pairs={{0,4},{1,17},{2,6},{3,19},{4,0},{5,21},{6,2},{7,23},{8,12},{9,25},... | collective-permute-start | bytes 12296 | tf_op jit(solution)/shard_map/ppermute | solution.py:583
  97.9 5.1 %collective-permute-start.29 = (f32[1,1024]{1,0:T(1,128)S(1)}, f32[1,1024]{1,0:T(1,128)S(1)}, u32[]{:S(2)}, u32[]{:S(2)}) collective-permute-start(f32[1,1024]{1,0:T(1,128)S(1)} %add.26), channel_id=1, source_target_pairs={{0,16},{1,5},{2,18},{3,7},{4,20},{5,1},{6,22},{7,3},{8,24},{9,13},... | collective-permute-start | bytes 12296 | tf_op jit(solution)/shard_map/ppermute | solution.py:583
  120.4 16.9 %collective-permute-start.32 = (f32[4,80,256]{2,1,0:T(8,128)S(1)}, f32[4,80,256]{2,1,0:T(8,128)S(1)}, u32[]{:S(2)}, u32[]{:S(2)}) collective-permute-start(f32[4,80,256]{2,1,0:T(8,128)S(1)} %get-tuple-element.98), channel_id=1, source_target_pairs={{0,8},{1,3},{2,10},{3,5},{4,12},{5,7},{6,14},{7,1},{8,16},{9,11},{... | collective-permute-start | bytes 983048 | tf_op jit(solution)/shard_map/ppermute | solution.py:576
  121.5 15.8 %collective-permute-start.33 = (f32[4,80,256]{2,1,0:T(8,128)S(1)}, f32[4,80,256]{2,1,0:T(8,128)S(1)}, u32[]{:S(2)}, u32[]{:S(2)}) collective-permute-start(f32[4,80,256]{2,1,0:T(8,128)S(1)} %get-tuple-element.99), channel_id=1, source_target_pairs={{0,24},{1,7},{2,26},{3,1},{4,28},{5,3},{6,30},{7,5},{8,0},{9,15},{... | collective-permute-start | bytes 983048 | tf_op jit(solution)/shard_map/ppermute | solution.py:576
  123.7 13.6 %collective-permute-start.34 = (f32[4,80,256]{2,1,0:T(8,128)S(1)}, f32[4,80,256]{2,1,0:T(8,128)S(1)}, u32[]{:S(2)}, u32[]{:S(2)}) collective-permute-start(f32[4,80,256]{2,1,0:T(8,128)S(1)} %get-tuple-element.100), channel_id=1, source_target_pairs={{0,16},{1,5},{2,18},{3,7},{4,20},{5,1},{6,22},{7,3},{8,24},{9,13},... | collective-permute-start | bytes 983048 | tf_op jit(solution)/shard_map/ppermute | solution.py:576
  137.4 18.6 %collective-permute-start.35 = (f32[80,256]{1,0:T(8,128)S(1)}, f32[80,256]{1,0:T(8,128)S(1)}, u32[]{:S(2)}, u32[]{:S(2)}) collective-permute-start(f32[80,256]{1,0:T(8,128)S(1)} %get-tuple-element.115), channel_id=1, source_target_pairs={{0,2},{1,9},{2,4},{3,11},{4,6},{5,13},{6,0},{7,15},{8,10},{9,17},{... | collective-permute-start | bytes 245768 | tf_op jit(solution)/shard_map/ppermute | solution.py:576
  139.5 16.5 %collective-permute-start.36 = (f32[80,256]{1,0:T(8,128)S(1)}, f32[80,256]{1,0:T(8,128)S(1)}, u32[]{:S(2)}, u32[]{:S(2)}) collective-permute-start(f32[80,256]{1,0:T(8,128)S(1)} %get-tuple-element.116), channel_id=1, source_target_pairs={{0,6},{1,25},{2,0},{3,27},{4,2},{5,29},{6,4},{7,31},{8,14},{9,1},{... | collective-permute-start | bytes 245768 | tf_op jit(solution)/shard_map/ppermute | solution.py:576
  140.7 15.3 %collective-permute-start.37 = (f32[80,256]{1,0:T(8,128)S(1)}, f32[80,256]{1,0:T(8,128)S(1)}, u32[]{:S(2)}, u32[]{:S(2)}) collective-permute-start(f32[80,256]{1,0:T(8,128)S(1)} %get-tuple-element.117), channel_id=1, source_target_pairs={{0,4},{1,17},{2,6},{3,19},{4,0},{5,21},{6,2},{7,23},{8,12},{9,25},... | collective-permute-start | bytes 245768 | tf_op jit(solution)/shard_map/ppermute | solution.py:576
  (7 other events, 29.5 us)
where the time goes:
time: 158 us; the launch traced here: 157 us
  Pallas kernels  69.7 us (44%)
  starting transfers between devices  52.5 us (33%)
  waiting for transfers between devices  30.3 us (19%)
  other arithmetic  2.97 us (2%)
    ppermute x15, starting transfers between devices, fetch(): lax.ppermute(value, EVERY, route_by(lambda x, z, y, c: along(axis, c, -by...  28.6 us
    pallas_call x2, Pallas kernels, table_grads(): pl.pallas_call(functools.partial(table_grad_kernel, width, fresh), grid=(...  27.1 us
    pallas_call x3, Pallas kernels, logits_call(): pl.pallas_call(functools.partial(logit_kernel, blocks, fresh), grid=(step...  25.7 us
    ppermute x15, waiting for transfers between devices, fetch(): lax.ppermute(value, EVERY, route_by(lambda x, z, y, c: along(axis, c, -by...  14.5 us
    pallas_call x1, Pallas kernels, per_device(): pl.pallas_call(hidden_grad_kernel, in_specs=[smem()] + [vmem()] * 5, out_...  11.9 us
    ppermute x4, waiting for transfers between devices, exchange(): return lax.ppermute(value, EVERY, route_by(other))  10.9 us
    ppermute x6, starting transfers between devices, hand_on(): lax.ppermute(value, EVERY, route_by(lambda x, z, y, c: along(axis, c, by,...  8.36 us
    ppermute x4, starting transfers between devices, exchange(): return lax.ppermute(value, EVERY, route_by(other))  7.25 us
  transfers between devices with their start and end apart: 38, of which 13 were waited for; matrix products, arithmetic and copies ran while one was open for 2% of the time, Pallas kernels for 35%

commit v1 on v0

--- a/solution.py
+++ b/solution.py
@@ -17,6 +17,7 @@
 LONG_STEP = 2000
 PADDED = 4096
 STRIP = 16
+WIDE_STRIP = 32
 GRAD_TILE = 512
 TABLE_TILE = 256
 FAST_SLOTS = 4
@@ -63,7 +64,7 @@
 def teacher_kernel(rows, thin, near, far, cot, ids, prob, row_counts, column_counts, joined):
     _, z, y, core = here()
     offset = block_offset(rows, z, y, core)
-    top = ids.shape[1]
+    top = ids.shape[0]
     share = 8
     group = thin + 2 * share
     for side, source in ((core, near), (1 - core, far)):
@@ -84,8 +85,9 @@
         scores = flipped[:top]
         local = flipped[top:].astype(jnp.int32) - offset
         raised = jnp.exp(scores - jnp.max(scores, axis=0, keepdims=True))
-        ids[block] = local
-        prob[block] = raised / jnp.sum(raised, axis=0, keepdims=True)
+        lanes = slice(block * BLOCK, (block + 1) * BLOCK)
+        ids[:, lanes] = local
+        prob[:, lanes] = raised / jnp.sum(raised, axis=0, keepdims=True)
         size = GRAD_TILE if block == 0 else TABLE_TILE
         for tile in range(PADDED // size):
             first = tile * size
@@ -219,27 +221,30 @@
     return (share - target) * (1.0 - ratio * ratio)
 
 
-def logit_grads(squashed, grads, log_share, relative, chances, fast, term=None):
-    last = jnp.full((1, BLOCK), -1, jnp.int32)
+def first_slots(relative, chances, fast):
+    last = jnp.full((1, relative.shape[1]), -1, jnp.int32)
     slots = []
     for _ in range(fast):
         last, chance = next_slot(relative, chances, last)
         slots.append((last, chance * LOSS_SCALE))
-    row = lax.broadcasted_iota(jnp.int32, (STRIP, BLOCK), 0)
+    return slots
+
+
+def logit_grads(squashed, grads, log_share, slots, lanes, term=None):
+    row = lax.broadcasted_iota(jnp.int32, (WIDE_STRIP, BLOCK), 0)
     added = jnp.zeros((8, BLOCK), jnp.float32)
-    for start in range(0, grads.shape[0], STRIP):
-        strip = slice(start, start + STRIP)
+    for start in range(0, grads.shape[0], WIDE_STRIP):
+        strip = slice(start, start + WIDE_STRIP)
         ratio = squashed[strip]
-        target = jnp.zeros((STRIP, BLOCK), jnp.float32)
+        target = jnp.zeros((WIDE_STRIP, BLOCK), jnp.float32)
         for where, value in slots:
-            target = jnp.where(row + start == where, value, target)
+            target = jnp.where(row + start == where[:, lanes], value[:, lanes], target)
         grads[strip] = gradient(ratio, target, log_share).astype(jnp.bfloat16)
         if term is not None:
             product = target * ratio
-            added = added + (product[:8] + product[8:])
+            added = added + jnp.sum(product.reshape(WIDE_STRIP // 8, 8, BLOCK), axis=0)
     if term is not None:
         term[...] += added
-    return last
 
 
 def more_targets(
@@ -300,8 +305,8 @@
         rows = rows_of(tile)
         rows_grad[...] += dot_tn(ready[...], embed[rows_of(jnp.maximum(tile - 1, 0))])
         held = squashed.at[rows]
-        relative = ids[0] - tile * GRAD_TILE
-        last = logit_grads(held, made, log_share, relative, prob[0], HIDDEN_SLOTS, term)
+        slots = first_slots(ids[:, 0:BLOCK] - tile * GRAD_TILE, prob[:, 0:BLOCK], HIDDEN_SLOTS)
+        logit_grads(held, made, log_share, slots, slice(0, BLOCK), term)
 
         @pl.when(counts[tile] > HIDDEN_SLOTS)
         def _():
@@ -309,9 +314,9 @@
                 held,
                 made,
                 log_share,
-                ids[0] - tile * GRAD_TILE,
-                prob[0],
-                last,
+                ids[:, 0:BLOCK] - tile * GRAD_TILE,
+                prob[:, 0:BLOCK],
+                slots[-1][0],
                 HIDDEN_SLOTS,
                 counts[tile],
                 term,
@@ -433,21 +438,32 @@
         made[:, 0:BLOCK] = own_grads[rows]
         made[:, 4 * BLOCK :] = onehot(tile, 0)
 
+        relative = ids[:, BLOCK:] - tile * TABLE_TILE
+        chances = prob[:, BLOCK:]
+        slots = first_slots(relative, chances, FAST_SLOTS)
+
         def of(block):
             lanes = pl.ds(block * BLOCK, BLOCK)
             held = far_squashed.at[rows] if block == 2 else side_squashed.at[rows, lanes]
             into = pl.ds((block + 1) * BLOCK, BLOCK)
-            log_share = jnp.log2(LOSS_SCALE / total[:, into])
-            relative = ids[block + 1] - tile * TABLE_TILE
-            return held, made.at[:, into], log_share, relative, prob[block + 1]
-
-        lasts = [logit_grads(*of(block), FAST_SLOTS) for block in range(blocks)]
+            return held, made.at[:, into], jnp.log2(LOSS_SCALE / total[:, into])
+
+        for block in range(blocks):
+            logit_grads(*of(block), slots, slice(block * BLOCK, (block + 1) * BLOCK))
         for block in range(blocks):
             count = counts[tile * blocks + block]
 
             @pl.when(count > FAST_SLOTS)
             def _(block=block, count=count):
-                more_targets(*of(block), lasts[block], FAST_SLOTS, count)
+                own = pl.ds((block + 1) * BLOCK, BLOCK)
+                more_targets(
+                    *of(block),
+                    ids[:, own] - tile * TABLE_TILE,
+                    prob[:, own],
+                    slots[-1][0][:, block * BLOCK : (block + 1) * BLOCK],
+                    FAST_SLOTS,
+                    count,
+                )
 
         @pl.when((chunks[0] > 1) & (index > 0))
         def _():
@@ -707,8 +723,8 @@
         "teacher_prep",
         [
             ((width, BLOCK), jnp.float32, vmem),
-            ((dp, top, BLOCK), jnp.int32, vmem),
-            ((dp, top, BLOCK), jnp.float32, vmem),
+            ((top, tokens), jnp.int32, vmem),
+            ((top, tokens), jnp.float32, vmem),
             ((PADDED // GRAD_TILE,), jnp.int32, smem),
             ((PADDED // TABLE_TILE * (dp - 1),), jnp.int32, smem),
         ],

time: 158 us -> 158 us (level)
  no operation moved by 1% of the time
where the time goes in v1:
time: 158 us; the launch traced here: 157 us
  Pallas kernels  69.8 us (44%)
  starting transfers between devices  52.5 us (33%)
  waiting for transfers between devices  30.3 us (19%)
  other arithmetic  2.97 us (2%)
    ppermute x15, starting transfers between devices, fetch(): lax.ppermute(value, EVERY, route_by(lambda x, z, y, c: along(axis, c, -by...  28.6 us
    pallas_call x2, Pallas kernels, table_grads(): pl.pallas_call(functools.partial(table_grad_kernel, width, fresh), grid=(...  27.1 us
    pallas_call x3, Pallas kernels, logits_call(): pl.pallas_call(functools.partial(logit_kernel, blocks, fresh), grid=(step...  25.7 us
    ppermute x15, waiting for transfers between devices, fetch(): lax.ppermute(value, EVERY, route_by(lambda x, z, y, c: along(axis, c, -by...  14.5 us
    pallas_call x1, Pallas kernels, per_device(): pl.pallas_call(hidden_grad_kernel, in_specs=[smem()] + [vmem()] * 5, out_...  12 us
    ppermute x4, waiting for transfers between devices, exchange(): return lax.ppermute(value, EVERY, route_by(other))  10.9 us
    ppermute x6, starting transfers between devices, hand_on(): lax.ppermute(value, EVERY, route_by(lambda x, z, y, c: along(axis, c, by,...  8.36 us
    ppermute x4, starting transfers between devices, exchange(): return lax.ppermute(value, EVERY, route_by(other))  7.25 us
  transfers between devices with their start and end apart: 38, of which 13 were waited for; matrix products, arithmetic and copies ran while one was open for 2% of the time, Pallas kernels for 35%

profile of v1, /device:TPU:0, one launch (start us, length us, event | category | flops | bytes accessed | tf_op | source)
XLA Modules:
  0.0 157.4 jit_solution(15696573892090266211)
XLA Ops:
  3.0 3.2 %collective-permute-start.1 = (bf16[144,128]{1,0:T(8,128)(2,1)S(1)}, bf16[144,128]{1,0:T(8,128)(2,1)S(1)}, u32[]{:S(2)}, u32[]{:S(2)}) collective-permute-start(bf16[144,128]{1,0:T(8,128)(2,1)S(1)} %get-tuple-element.122), channel_id=1, source_target_pairs={{0,6},{1,25},{2,0},{3,27},{4,2},{5,29},{6,4},{7,31},{8,14},{9,1},{... | collective-permute-start | bytes 110600 | tf_op jit(solution)/shard_map/ppermute | solution.py:588
  6.1 2.2 %collective-permute-start.3 = (bf16[144,128]{1,0:T(8,128)(2,1)S(1)}, bf16[144,128]{1,0:T(8,128)(2,1)S(1)}, u32[]{:S(2)}, u32[]{:S(2)}) collective-permute-start(bf16[144,128]{1,0:T(8,128)(2,1)S(1)} %get-tuple-element.122), channel_id=1, source_target_pairs={{0,4},{1,17},{2,6},{3,19},{4,0},{5,21},{6,2},{7,23},{8,12},{9,25},... | collective-permute-start | bytes 110600 | tf_op jit(solution)/shard_map/ppermute | solution.py:588
  9.1 2.2 %collective-permute-done.2 = bf16[144,128]{1,0:T(8,128)(2,1)S(1)} collective-permute-done((bf16[144,128]{1,0:T(8,128)(2,1)S(1)}, bf16[144,128]{1,0:T(8,128)(2,1)S(1)}, u32[]{:S(2)}, u32[]{:S(2)}) %collective-permute-start.2) | collective-permute-done | bytes 36896 | tf_op jit(solution)/shard_map/ppermute | solution.py:588
  11.7 2.8 %collective-permute-start.8 = (f32[16,128]{1,0:T(8,128)S(1)}, f32[16,128]{1,0:T(8,128)S(1)}, u32[]{:S(2)}, u32[]{:S(2)}) collective-permute-start(f32[16,128]{1,0:T(8,128)S(1)} %maximum_maximum_fusion), channel_id=1, source_target_pairs={{32,0},{64,32},{96,64},{0,96},{33,1},{65,33},{97,65},{1,97},{34,2}... | collective-permute-start | bytes 24584 | tf_op jit(solution)/shard_map/ppermute | solution.py:642
  14.5 2.3 %collective-permute-start.9 = (f32[16,128]{1,0:T(8,128)S(1)}, f32[16,128]{1,0:T(8,128)S(1)}, u32[]{:S(2)}, u32[]{:S(2)}) collective-permute-start(f32[16,128]{1,0:T(8,128)S(1)} %maximum_maximum_fusion), channel_id=1, source_target_pairs={{64,0},{96,32},{0,64},{32,96},{65,1},{97,33},{1,65},{33,97},{66,2}... | collective-permute-start | bytes 24584 | tf_op jit(solution)/shard_map/ppermute | solution.py:642
  16.8 4.0 %collective-permute-start.4 = (bf16[576,128]{1,0:T(8,128)(2,1)S(1)}, bf16[576,128]{1,0:T(8,128)(2,1)S(1)}, u32[]{:S(2)}, u32[]{:S(2)}) collective-permute-start(bf16[576,128]{1,0:T(8,128)(2,1)S(1)} %pad_maximum_fusion), channel_id=1, source_target_pairs={{0,24},{1,7},{2,26},{3,1},{4,28},{5,3},{6,30},{7,5},{8,0},{9,15},{... | collective-permute-start | bytes 442376 | tf_op jit(solution)/shard_map/ppermute | solution.py:588
  20.9 1.9 %collective-permute-start.6 = (bf16[576,128]{1,0:T(8,128)(2,1)S(1)}, bf16[576,128]{1,0:T(8,128)(2,1)S(1)}, u32[]{:S(2)}, u32[]{:S(2)}) collective-permute-start(bf16[576,128]{1,0:T(8,128)(2,1)S(1)} %pad_maximum_fusion), channel_id=1, source_target_pairs={{0,16},{1,5},{2,18},{3,7},{4,20},{5,1},{6,22},{7,3},{8,24},{9,13},... | collective-permute-start | bytes 442376 | tf_op jit(solution)/shard_map/ppermute | solution.py:588
  24.4 4.4 %collective-permute-done.5 = bf16[576,128]{1,0:T(8,128)(2,1)S(1)} collective-permute-done((bf16[576,128]{1,0:T(8,128)(2,1)S(1)}, bf16[576,128]{1,0:T(8,128)(2,1)S(1)}, u32[]{:S(2)}, u32[]{:S(2)}) %collective-permute-start.5) | collective-permute-done | bytes 147488 | tf_op jit(solution)/shard_map/ppermute | solution.py:588
  29.0 4.7 %collective-permute-start.12 = (bf16[2304,128]{1,0:T(8,128)(2,1)S(1)}, bf16[2304,128]{1,0:T(8,128)(2,1)S(1)}, u32[]{:S(2)}, u32[]{:S(2)}) collective-permute-start(bf16[2304,128]{1,0:T(8,128)(2,1)S(1)} %constant_dynamic-update-slice_fusion.refs_0_), channel_id=1, source_target_pairs={{0,96},{1,33},{2,98},{3,35},{4,100},{5,37},{6,102},{7,39},{8,104},... | collective-permute-start | bytes 1769480 | tf_op jit(solution)/shard_map/ppermute | solution.py:588
  33.7 8.5 %logits_1.2 = (f32[4096,256]{1,0:T(8,128)S(1)}, f32[1,256]{1,0:T(1,128)S(1)}, bf16[1,576,256]{2,1,0:T(8,128)(2,1)S(1)}, bf16[4096,2304]{1,0:T(8,128)(2,1)S(1)}) custom-call(bf16[4000,2304]{1,0:T(8,128)(2,1)} %embed.1, bf16[2304,128]{1,0:T(8,128)(2,1)S(1)} %constant_dynamic-update-slice_fusion.refs_0_, bf16[2304,128]{1,0:T(8,128)(2,1)S(1)} %collective-permute-done.11.refs_1_), custom_call_target="tpu_custom_call" | custom-call | flops 4718592000 | bytes 22528000 | tf_op jit(solution)/shard_map/logits_1/pallas_call | solution.py:544
  43.5 3.4 %collective-permute-done.12.refs_0_ = bf16[2304,128]{1,0:T(8,128)(2,1)S(1)} collective-permute-done((bf16[2304,128]{1,0:T(8,128)(2,1)S(1)}, bf16[2304,128]{1,0:T(8,128)(2,1)S(1)}, u32[]{:S(2)}, u32[]{:S(2)}) %collective-permute-start.12) | collective-permute-done | bytes 589856 | tf_op jit(solution)/shard_map/ppermute | solution.py:588
  48.1 3.0 %collective-permute-start.18 = (bf16[2304,128]{1,0:T(8,128)(2,1)S(1)}, bf16[2304,128]{1,0:T(8,128)(2,1)S(1)}, u32[]{:S(2)}, u32[]{:S(2)}) collective-permute-start(bf16[2304,128]{1,0:T(8,128)(2,1)S(1)} %collective-permute-done.12.refs_0_), channel_id=1, source_target_pairs={{0,96},{1,33},{2,98},{3,35},{4,100},{5,37},{6,102},{7,39},{8,104},... | collective-permute-start | bytes 1769480 | tf_op jit(solution)/shard_map/ppermute | solution.py:588
  51.1 3.1 %collective-permute-start.15 = (f32[176,128]{1,0:T(8,128)S(1)}, f32[176,128]{1,0:T(8,128)S(1)}, u32[]{:S(2)}, u32[]{:S(2)}) collective-permute-start(f32[176,128]{1,0:T(8,128)S(1)} %maximum_select_fusion), channel_id=1, source_target_pairs={{0,6},{1,25},{2,0},{3,27},{4,2},{5,29},{6,4},{7,31},{8,14},{9,1},{... | collective-permute-start | bytes 270344 | tf_op jit(solution)/shard_map/ppermute | solution.py:588
  55.7 11.3 %logits_2.1 = (f32[4096,512]{1,0:T(8,128)S(1)}, f32[1,512]{1,0:T(1,128)S(1)}, bf16[2,576,256]{2,1,0:T(8,128)(2,1)S(1)}) custom-call(bf16[4096,2304]{1,0:T(8,128)(2,1)S(1)} %get-tuple-element.71.embed, bf16[2304,128]{1,0:T(8,128)(2,1)S(1)} %collective-permute-done.12.refs_0_, bf16[2304,128]{1,0:T(8,128)(2,1)S(1)} %collective-permute-done.13.refs_1_, ...), custom_call_target="tpu_custom_call" | custom-call | flops 9663676416 | bytes 8388608 | tf_op jit(solution)/shard_map/logits_2/pallas_call | solution.py:544
  67.5 2.7 %collective-permute-start.22 = (f32[704,128]{1,0:T(8,128)S(1)}, f32[704,128]{1,0:T(8,128)S(1)}, u32[]{:S(2)}, u32[]{:S(2)}) collective-permute-start(f32[704,128]{1,0:T(8,128)S(1)} %constant_dynamic-update-slice_fusion.7), channel_id=1, source_target_pairs={{0,8},{1,3},{2,10},{3,5},{4,12},{5,7},{6,14},{7,1},{8,16},{9,11},{... | collective-permute-start | bytes 1081352 | tf_op jit(solution)/shard_map/ppermute | solution.py:588
  70.2 2.0 %collective-permute-start.23 = (f32[704,128]{1,0:T(8,128)S(1)}, f32[704,128]{1,0:T(8,128)S(1)}, u32[]{:S(2)}, u32[]{:S(2)}) collective-permute-start(f32[704,128]{1,0:T(8,128)S(1)} %constant_dynamic-update-slice_fusion.7), channel_id=1, source_target_pairs={{0,16},{1,5},{2,18},{3,7},{4,20},{5,1},{6,22},{7,3},{8,24},{9,13},... | collective-permute-start | bytes 1081352 | tf_op jit(solution)/shard_map/ppermute | solution.py:588
  72.2 5.9 %logits_1.3 = (f32[4096,256]{1,0:T(8,128)S(1)}, f32[1,256]{1,0:T(1,128)S(1)}, bf16[1,576,256]{2,1,0:T(8,128)(2,1)S(1)}) custom-call(bf16[4096,2304]{1,0:T(8,128)(2,1)S(1)} %get-tuple-element.71.embed, bf16[2304,128]{1,0:T(8,128)(2,1)S(1)} %collective-permute-done.18.refs_0_, bf16[2304,128]{1,0:T(8,128)(2,1)S(1)} %collective-permute-done.24.refs_1_), custom_call_target="tpu_custom_call" | custom-call | flops 4831838208 | bytes 4194304 | tf_op jit(solution)/shard_map/logits_1/pallas_call | solution.py:544
  78.1 3.3 %collective-permute-done.23 = f32[704,128]{1,0:T(8,128)S(1)} collective-permute-done((f32[704,128]{1,0:T(8,128)S(1)}, f32[704,128]{1,0:T(8,128)S(1)}, u32[]{:S(2)}, u32[]{:S(2)}) %collective-permute-start.23) | collective-permute-done | bytes 360480 | tf_op jit(solution)/shard_map/ppermute | solution.py:588
  82.3 2.6 %collective-permute-done.25 = f32[1,1024]{1,0:T(1,128)S(1)} collective-permute-done((f32[1,1024]{1,0:T(1,128)S(1)}, f32[1,1024]{1,0:T(1,128)S(1)}, u32[]{:S(2)}, u32[]{:S(2)}) %collective-permute-start.25) | collective-permute-done | bytes 4128 | tf_op jit(solution)/shard_map/ppermute | solution.py:603
  84.9 2.7 %collective-permute-start.26 = (f32[1,1024]{1,0:T(1,128)S(1)}, f32[1,1024]{1,0:T(1,128)S(1)}, u32[]{:S(2)}, u32[]{:S(2)}) collective-permute-start(f32[1,1024]{1,0:T(1,128)S(1)} %maximum_add_fusion), channel_id=1, source_target_pairs={{0,2},{1,9},{2,0},{3,11},{4,6},{5,13},{6,4},{7,15},{8,10},{9,1},{1... | collective-permute-start | bytes 12296 | tf_op jit(solution)/shard_map/ppermute | solution.py:599
  87.6 1.6 %collective-permute-done.26 = f32[1,1024]{1,0:T(1,128)S(1)} collective-permute-done((f32[1,1024]{1,0:T(1,128)S(1)}, f32[1,1024]{1,0:T(1,128)S(1)}, u32[]{:S(2)}, u32[]{:S(2)}) %collective-permute-start.26) | collective-permute-done | bytes 4128 | tf_op jit(solution)/shard_map/ppermute | solution.py:599
  90.7 3.7 %collective-permute-done.27 = f32[1,1024]{1,0:T(1,128)S(1)} collective-permute-done((f32[1,1024]{1,0:T(1,128)S(1)}, f32[1,1024]{1,0:T(1,128)S(1)}, u32[]{:S(2)}, u32[]{:S(2)}) %collective-permute-start.27) | collective-permute-done | bytes 4128 | tf_op jit(solution)/shard_map/ppermute | solution.py:599
  95.4 2.6 %collective-permute-done.28 = f32[1,1024]{1,0:T(1,128)S(1)} collective-permute-done((f32[1,1024]{1,0:T(1,128)S(1)}, f32[1,1024]{1,0:T(1,128)S(1)}, u32[]{:S(2)}, u32[]{:S(2)}) %collective-permute-start.28) | collective-permute-done | bytes 4128 | tf_op jit(solution)/shard_map/ppermute | solution.py:599
  97.9 2.0 %collective-permute-start.29 = (f32[1,1024]{1,0:T(1,128)S(1)}, f32[1,1024]{1,0:T(1,128)S(1)}, u32[]{:S(2)}, u32[]{:S(2)}) collective-permute-start(f32[1,1024]{1,0:T(1,128)S(1)} %add.26), channel_id=1, source_target_pairs={{0,16},{1,5},{2,18},{3,7},{4,20},{5,1},{6,22},{7,3},{8,24},{9,13},... | collective-permute-start | bytes 12296 | tf_op jit(solution)/shard_map/ppermute | solution.py:599
  100.0 3.1 %collective-permute-done.29 = f32[1,1024]{1,0:T(1,128)S(1)} collective-permute-done((f32[1,1024]{1,0:T(1,128)S(1)}, f32[1,1024]{1,0:T(1,128)S(1)}, u32[]{:S(2)}, u32[]{:S(2)}) %collective-permute-start.29) | collective-permute-done | bytes 4128 | tf_op jit(solution)/shard_map/ppermute | solution.py:599
  103.1 2.2 %teacher_prep.1 = (f32[2304,256]{1,0:T(8,128)S(1)}, s32[64,1024]{1,0:T(8,128)S(1)}, f32[64,1024]{1,0:T(8,128)S(1)}, s32[8]{0:T(128)S(1)}, s32[48]{0:T(128)S(1)}) custom-call(f32[2816,128]{1,0:T(8,128)S(1)} %constant_dynamic-update-slice_fusion.14.near, f32[2816,128]{1,0:T(8,128)S(1)} %collective-permute-done.30.far), custom_call_target="tpu_custom_call" | custom-call | tf_op jit(solution)/shard_map/teacher_prep/pallas_call | solution.py:508
  105.2 12.0 %hidden_grads.1 = (bf16[4096,256]{1,0:T(8,128)(2,1)S(1)}, f32[4,4,80,256]{3,2,1,0:T(8,128)S(1)}, f32[4,4,80,256]{3,2,1,0:T(8,128)S(1)}) custom-call(s32[8]{0:T(128)S(1)} %get-tuple-element.86.counts, bf16[4096,2304]{1,0:T(8,128)(2,1)S(1)} %get-tuple-element.71.embed, f32[4096,256]{1,0:T(8,128)S(1)} %get-tuple-element.87.squashed, f32[1,1024]{1,0:T(1,128)S(1)} %add.27.total, ...), custom_call_target="tpu_custom_call" | custom-call | flops 4718592000 | bytes 6144000 | tf_op jit(solution)/shard_map/hidden_grads/pallas_call | solution.py:749
  117.4 1.8 %lookup_prep.1 = (bf16[4,576,256]{2,1,0:T(8,128)(2,1)S(1)}, s32[4,1,256]{2,1,0:T(1,128)S(1)}, s32[1]{0:T(128)}) custom-call(f32[4,16,128]{2,1,0:T(8,128)S(1)} %pad_maximum_fusion.3.packs, f32[2304,256]{1,0:T(8,128)S(1)} %get-tuple-element.93.cot), custom_call_target="tpu_custom_call" | custom-call | tf_op jit(solution)/shard_map/lookup_prep/pallas_call | solution.py:508
  121.7 2.2 %collective-permute-start.33 = (f32[4,80,256]{2,1,0:T(8,128)S(1)}, f32[4,80,256]{2,1,0:T(8,128)S(1)}, u32[]{:S(2)}, u32[]{:S(2)}) collective-permute-start(f32[4,80,256]{2,1,0:T(8,128)S(1)} %get-tuple-element.99), channel_id=1, source_target_pairs={{0,24},{1,7},{2,26},{3,1},{4,28},{5,3},{6,30},{7,5},{8,0},{9,15},{... | collective-permute-start | bytes 983048 | tf_op jit(solution)/shard_map/ppermute | solution.py:592
  124.7 12.7 %table_grads_start.1.refs_0_ = bf16[576,2048]{1,0:T(8,128)(2,1)S(1)} custom-call(s32[48]{0:T(128)S(1)} %get-tuple-element.101.counts, s32[1]{0:T(128)} %get-tuple-element.102.chunks, bf16[4096,256]{1,0:T(8,128)(2,1)S(1)} %get-tuple-element.103.own_grads, f32[4096,512]{1,0:T(8,128)S(1)} %get-tuple-element.104.side_squashed, ...), custom_call_target="tpu_custom_call" | custom-call | flops 3019898880 | bytes 4608000 | tf_op jit(solution)/shard_map/table_grads_start/pallas_call | solution.py:794
  137.5 2.1 %collective-permute-start.35 = (f32[80,256]{1,0:T(8,128)S(1)}, f32[80,256]{1,0:T(8,128)S(1)}, u32[]{:S(2)}, u32[]{:S(2)}) collective-permute-start(f32[80,256]{1,0:T(8,128)S(1)} %get-tuple-element.115), channel_id=1, source_target_pairs={{0,2},{1,9},{2,4},{3,11},{4,6},{5,13},{6,0},{7,15},{8,10},{9,17},{... | collective-permute-start | bytes 245768 | tf_op jit(solution)/shard_map/ppermute | solution.py:592
  141.8 14.3 %table_grads_rest.1 = bf16[576,4000]{1,0:T(8,128)(2,1)} custom-call(s32[48]{0:T(128)S(1)} %get-tuple-element.101.counts, s32[1]{0:T(128)} %get-tuple-element.102.chunks, bf16[4096,256]{1,0:T(8,128)(2,1)S(1)} %get-tuple-element.103.own_grads, f32[4096,512]{1,0:T(8,128)S(1)} %get-tuple-element.104.side_squashed, ...), custom_call_target="tpu_custom_call" | custom-call | flops 3019898880 | bytes 4608000 | tf_op jit(solution)/shard_map/table_grads_rest/pallas_call | solution.py:794
  (97 shorter events, 19.9 us)
Async XLA Ops:
  3.0 6.1 %collective-permute-start.1 = (bf16[144,128]{1,0:T(8,128)(2,1)S(1)}, bf16[144,128]{1,0:T(8,128)(2,1)S(1)}, u32[]{:S(2)}, u32[]{:S(2)}) collective-permute-start(bf16[144,128]{1,0:T(8,128)(2,1)S(1)} %get-tuple-element.122), channel_id=1, source_target_pairs={{0,6},{1,25},{2,0},{3,27},{4,2},{5,29},{6,4},{7,31},{8,14},{9,1},{... | collective-permute-start | bytes 110600 | tf_op jit(solution)/shard_map/ppermute | solution.py:588
  6.1 5.2 %collective-permute-start.2 = (bf16[144,128]{1,0:T(8,128)(2,1)S(1)}, bf16[144,128]{1,0:T(8,128)(2,1)S(1)}, u32[]{:S(2)}, u32[]{:S(2)}) collective-permute-start(bf16[144,128]{1,0:T(8,128)(2,1)S(1)} %get-tuple-element.122), channel_id=1, source_target_pairs={{0,2},{1,9},{2,4},{3,11},{4,6},{5,13},{6,0},{7,15},{8,10},{9,17},{... | collective-permute-start | bytes 110600 | tf_op jit(solution)/shard_map/ppermute | solution.py:588
  6.1 5.6 %collective-permute-start.3 = (bf16[144,128]{1,0:T(8,128)(2,1)S(1)}, bf16[144,128]{1,0:T(8,128)(2,1)S(1)}, u32[]{:S(2)}, u32[]{:S(2)}) collective-permute-start(bf16[144,128]{1,0:T(8,128)(2,1)S(1)} %get-tuple-element.122), channel_id=1, source_target_pairs={{0,4},{1,17},{2,6},{3,19},{4,0},{5,21},{6,2},{7,23},{8,12},{9,25},... | collective-permute-start | bytes 110600 | tf_op jit(solution)/shard_map/ppermute | solution.py:588
  11.7 9.2 %collective-permute-start.8 = (f32[16,128]{1,0:T(8,128)S(1)}, f32[16,128]{1,0:T(8,128)S(1)}, u32[]{:S(2)}, u32[]{:S(2)}) collective-permute-start(f32[16,128]{1,0:T(8,128)S(1)} %maximum_maximum_fusion), channel_id=1, source_target_pairs={{32,0},{64,32},{96,64},{0,96},{33,1},{65,33},{97,65},{1,97},{34,2}... | collective-permute-start | bytes 24584 | tf_op jit(solution)/shard_map/ppermute | solution.py:642
  14.5 8.3 %collective-permute-start.10 = (f32[16,128]{1,0:T(8,128)S(1)}, f32[16,128]{1,0:T(8,128)S(1)}, u32[]{:S(2)}, u32[]{:S(2)}) collective-permute-start(f32[16,128]{1,0:T(8,128)S(1)} %maximum_maximum_fusion), channel_id=1, source_target_pairs={{96,0},{0,32},{32,64},{64,96},{97,1},{1,33},{33,65},{65,97},{98,2}... | collective-permute-start | bytes 24584 | tf_op jit(solution)/shard_map/ppermute | solution.py:642
  14.5 9.7 %collective-permute-start.9 = (f32[16,128]{1,0:T(8,128)S(1)}, f32[16,128]{1,0:T(8,128)S(1)}, u32[]{:S(2)}, u32[]{:S(2)}) collective-permute-start(f32[16,128]{1,0:T(8,128)S(1)} %maximum_maximum_fusion), channel_id=1, source_target_pairs={{64,0},{96,32},{0,64},{32,96},{65,1},{97,33},{1,65},{33,97},{66,2}... | collective-permute-start | bytes 24584 | tf_op jit(solution)/shard_map/ppermute | solution.py:642
  16.8 7.5 %collective-permute-start.4 = (bf16[576,128]{1,0:T(8,128)(2,1)S(1)}, bf16[576,128]{1,0:T(8,128)(2,1)S(1)}, u32[]{:S(2)}, u32[]{:S(2)}) collective-permute-start(bf16[576,128]{1,0:T(8,128)(2,1)S(1)} %pad_maximum_fusion), channel_id=1, source_target_pairs={{0,24},{1,7},{2,26},{3,1},{4,28},{5,3},{6,30},{7,5},{8,0},{9,15},{... | collective-permute-start | bytes 442376 | tf_op jit(solution)/shard_map/ppermute | solution.py:588
  20.9 7.9 %collective-permute-start.5 = (bf16[576,128]{1,0:T(8,128)(2,1)S(1)}, bf16[576,128]{1,0:T(8,128)(2,1)S(1)}, u32[]{:S(2)}, u32[]{:S(2)}) collective-permute-start(bf16[576,128]{1,0:T(8,128)(2,1)S(1)} %pad_maximum_fusion), channel_id=1, source_target_pairs={{0,8},{1,3},{2,10},{3,5},{4,12},{5,7},{6,14},{7,1},{8,16},{9,11},{... | collective-permute-start | bytes 442376 | tf_op jit(solution)/shard_map/ppermute | solution.py:588
  20.9 7.9 %collective-permute-start.6 = (bf16[576,128]{1,0:T(8,128)(2,1)S(1)}, bf16[576,128]{1,0:T(8,128)(2,1)S(1)}, u32[]{:S(2)}, u32[]{:S(2)}) collective-permute-start(bf16[576,128]{1,0:T(8,128)(2,1)S(1)} %pad_maximum_fusion), channel_id=1, source_target_pairs={{0,16},{1,5},{2,18},{3,7},{4,20},{5,1},{6,22},{7,3},{8,24},{9,13},... | collective-permute-start | bytes 442376 | tf_op jit(solution)/shard_map/ppermute | solution.py:588
  28.9 4.8 %collective-permute-start.11 = (bf16[2304,128]{1,0:T(8,128)(2,1)S(1)}, bf16[2304,128]{1,0:T(8,128)(2,1)S(1)}, u32[]{:S(2)}, u32[]{:S(2)}) collective-permute-start(bf16[2304,128]{1,0:T(8,128)(2,1)S(1)} %constant_dynamic-update-slice_fusion.refs_0_), channel_id=1, source_target_pairs={{0,1},{1,0},{2,3},{3,2},{4,5},{5,4},{6,7},{7,6},{8,9},{9,8},{10,11... | collective-permute-start | bytes 1769480 | tf_op jit(solution)/shard_map/ppermute | solution.py:603
  29.0 17.9 %collective-permute-start.12 = (bf16[2304,128]{1,0:T(8,128)(2,1)S(1)}, bf16[2304,128]{1,0:T(8,128)(2,1)S(1)}, u32[]{:S(2)}, u32[]{:S(2)}) collective-permute-start(bf16[2304,128]{1,0:T(8,128)(2,1)S(1)} %constant_dynamic-update-slice_fusion.refs_0_), channel_id=1, source_target_pairs={{0,96},{1,33},{2,98},{3,35},{4,100},{5,37},{6,102},{7,39},{8,104},... | collective-permute-start | bytes 1769480 | tf_op jit(solution)/shard_map/ppermute | solution.py:588
  33.7 13.9 %collective-permute-start.13 = (bf16[2304,128]{1,0:T(8,128)(2,1)S(1)}, bf16[2304,128]{1,0:T(8,128)(2,1)S(1)}, u32[]{:S(2)}, u32[]{:S(2)}) collective-permute-start(bf16[2304,128]{1,0:T(8,128)(2,1)S(1)} %constant_dynamic-update-slice_fusion.refs_0_), channel_id=1, source_target_pairs={{0,32},{1,97},{2,34},{3,99},{4,36},{5,101},{6,38},{7,103},{8,40},{... | collective-permute-start | bytes 1769480 | tf_op jit(solution)/shard_map/ppermute | solution.py:588
  47.6 6.6 %collective-permute-start.19 = (bf16[2304,128]{1,0:T(8,128)(2,1)S(1)}, bf16[2304,128]{1,0:T(8,128)(2,1)S(1)}, u32[]{:S(2)}, u32[]{:S(2)}) collective-permute-start(bf16[2304,128]{1,0:T(8,128)(2,1)S(1)} %collective-permute-done.13.refs_1_), channel_id=1, source_target_pairs={{0,1},{1,0},{2,3},{3,2},{4,5},{5,4},{6,7},{7,6},{8,9},{9,8},{10,11... | collective-permute-start | bytes 1769480 | tf_op jit(solution)/shard_map/ppermute | solution.py:603
  47.6 8.1 %collective-permute-start.20 = (bf16[2304,128]{1,0:T(8,128)(2,1)S(1)}, bf16[2304,128]{1,0:T(8,128)(2,1)S(1)}, u32[]{:S(2)}, u32[]{:S(2)}) collective-permute-start(bf16[2304,128]{1,0:T(8,128)(2,1)S(1)} %collective-permute-done.12.refs_0_), channel_id=1, source_target_pairs={{0,1},{1,0},{2,3},{3,2},{4,5},{5,4},{6,7},{7,6},{8,9},{9,8},{10,11... | collective-permute-start | bytes 1769480 | tf_op jit(solution)/shard_map/ppermute | solution.py:603
  48.1 19.0 %collective-permute-start.18 = (bf16[2304,128]{1,0:T(8,128)(2,1)S(1)}, bf16[2304,128]{1,0:T(8,128)(2,1)S(1)}, u32[]{:S(2)}, u32[]{:S(2)}) collective-permute-start(bf16[2304,128]{1,0:T(8,128)(2,1)S(1)} %collective-permute-done.12.refs_0_), channel_id=1, source_target_pairs={{0,96},{1,33},{2,98},{3,35},{4,100},{5,37},{6,102},{7,39},{8,104},... | collective-permute-start | bytes 1769480 | tf_op jit(solution)/shard_map/ppermute | solution.py:588
  51.1 15.9 %collective-permute-start.15 = (f32[176,128]{1,0:T(8,128)S(1)}, f32[176,128]{1,0:T(8,128)S(1)}, u32[]{:S(2)}, u32[]{:S(2)}) collective-permute-start(f32[176,128]{1,0:T(8,128)S(1)} %maximum_select_fusion), channel_id=1, source_target_pairs={{0,6},{1,25},{2,0},{3,27},{4,2},{5,29},{6,4},{7,31},{8,14},{9,1},{... | collective-permute-start | bytes 270344 | tf_op jit(solution)/shard_map/ppermute | solution.py:588
  54.2 12.8 %collective-permute-start.16 = (f32[176,128]{1,0:T(8,128)S(1)}, f32[176,128]{1,0:T(8,128)S(1)}, u32[]{:S(2)}, u32[]{:S(2)}) collective-permute-start(f32[176,128]{1,0:T(8,128)S(1)} %maximum_select_fusion), channel_id=1, source_target_pairs={{0,2},{1,9},{2,4},{3,11},{4,6},{5,13},{6,0},{7,15},{8,10},{9,17},{... | collective-permute-start | bytes 270344 | tf_op jit(solution)/shard_map/ppermute | solution.py:588
  54.2 12.8 %collective-permute-start.17 = (f32[176,128]{1,0:T(8,128)S(1)}, f32[176,128]{1,0:T(8,128)S(1)}, u32[]{:S(2)}, u32[]{:S(2)}) collective-permute-start(f32[176,128]{1,0:T(8,128)S(1)} %maximum_select_fusion), channel_id=1, source_target_pairs={{0,4},{1,17},{2,6},{3,19},{4,0},{5,21},{6,2},{7,23},{8,12},{9,25},... | collective-permute-start | bytes 270344 | tf_op jit(solution)/shard_map/ppermute | solution.py:588
  67.1 5.1 %collective-permute-start.24 = (bf16[2304,128]{1,0:T(8,128)(2,1)S(1)}, bf16[2304,128]{1,0:T(8,128)(2,1)S(1)}, u32[]{:S(2)}, u32[]{:S(2)}) collective-permute-start(bf16[2304,128]{1,0:T(8,128)(2,1)S(1)} %collective-permute-done.18.refs_0_), channel_id=1, source_target_pairs={{0,1},{1,0},{2,3},{3,2},{4,5},{5,4},{6,7},{7,6},{8,9},{9,8},{10,11... | collective-permute-start | bytes 1769480 | tf_op jit(solution)/shard_map/ppermute | solution.py:603
  67.2 10.9 %collective-permute-start.21 = (f32[704,128]{1,0:T(8,128)S(1)}, f32[704,128]{1,0:T(8,128)S(1)}, u32[]{:S(2)}, u32[]{:S(2)}) collective-permute-start(f32[704,128]{1,0:T(8,128)S(1)} %constant_dynamic-update-slice_fusion.7), channel_id=1, source_target_pairs={{0,24},{1,7},{2,26},{3,1},{4,28},{5,3},{6,30},{7,5},{8,0},{9,15},{... | collective-permute-start | bytes 1081352 | tf_op jit(solution)/shard_map/ppermute | solution.py:588
  67.5 10.6 %collective-permute-start.22 = (f32[704,128]{1,0:T(8,128)S(1)}, f32[704,128]{1,0:T(8,128)S(1)}, u32[]{:S(2)}, u32[]{:S(2)}) collective-permute-start(f32[704,128]{1,0:T(8,128)S(1)} %constant_dynamic-update-slice_fusion.7), channel_id=1, source_target_pairs={{0,8},{1,3},{2,10},{3,5},{4,12},{5,7},{6,14},{7,1},{8,16},{9,11},{... | collective-permute-start | bytes 1081352 | tf_op jit(solution)/shard_map/ppermute | solution.py:588
  70.2 11.2 %collective-permute-start.23 = (f32[704,128]{1,0:T(8,128)S(1)}, f32[704,128]{1,0:T(8,128)S(1)}, u32[]{:S(2)}, u32[]{:S(2)}) collective-permute-start(f32[704,128]{1,0:T(8,128)S(1)} %constant_dynamic-update-slice_fusion.7), channel_id=1, source_target_pairs={{0,16},{1,5},{2,18},{3,7},{4,20},{5,1},{6,22},{7,3},{8,24},{9,13},... | collective-permute-start | bytes 1081352 | tf_op jit(solution)/shard_map/ppermute | solution.py:588
  81.6 21.5 %collective-permute-start.30 = (f32[2816,128]{1,0:T(8,128)S(1)}, f32[2816,128]{1,0:T(8,128)S(1)}, u32[]{:S(2)}, u32[]{:S(2)}) collective-permute-start(f32[2816,128]{1,0:T(8,128)S(1)} %constant_dynamic-update-slice_fusion.14.near), channel_id=1, source_target_pairs={{0,1},{1,0},{2,3},{3,2},{4,5},{5,4},{6,7},{7,6},{8,9},{9,8},{10,11... | collective-permute-start | bytes 4325384 | tf_op jit(solution)/shard_map/ppermute | solution.py:603
  84.9 4.3 %collective-permute-start.26 = (f32[1,1024]{1,0:T(1,128)S(1)}, f32[1,1024]{1,0:T(1,128)S(1)}, u32[]{:S(2)}, u32[]{:S(2)}) collective-permute-start(f32[1,1024]{1,0:T(1,128)S(1)} %maximum_add_fusion), channel_id=1, source_target_pairs={{0,2},{1,9},{2,0},{3,11},{4,6},{5,13},{6,4},{7,15},{8,10},{9,1},{1... | collective-permute-start | bytes 12296 | tf_op jit(solution)/shard_map/ppermute | solution.py:599
  89.2 5.1 %collective-permute-start.27 = (f32[1,1024]{1,0:T(1,128)S(1)}, f32[1,1024]{1,0:T(1,128)S(1)}, u32[]{:S(2)}, u32[]{:S(2)}) collective-permute-start(f32[1,1024]{1,0:T(1,128)S(1)} %add.24), channel_id=1, source_target_pairs={{0,4},{1,17},{2,6},{3,19},{4,0},{5,21},{6,2},{7,23},{8,12},{9,25},... | collective-permute-start | bytes 12296 | tf_op jit(solution)/shard_map/ppermute | solution.py:599
  97.9 5.1 %collective-permute-start.29 = (f32[1,1024]{1,0:T(1,128)S(1)}, f32[1,1024]{1,0:T(1,128)S(1)}, u32[]{:S(2)}, u32[]{:S(2)}) collective-permute-start(f32[1,1024]{1,0:T(1,128)S(1)} %add.26), channel_id=1, source_target_pairs={{0,16},{1,5},{2,18},{3,7},{4,20},{5,1},{6,22},{7,3},{8,24},{9,13},... | collective-permute-start | bytes 12296 | tf_op jit(solution)/shard_map/ppermute | solution.py:599
  120.6 16.8 %collective-permute-start.32 = (f32[4,80,256]{2,1,0:T(8,128)S(1)}, f32[4,80,256]{2,1,0:T(8,128)S(1)}, u32[]{:S(2)}, u32[]{:S(2)}) collective-permute-start(f32[4,80,256]{2,1,0:T(8,128)S(1)} %get-tuple-element.98), channel_id=1, source_target_pairs={{0,8},{1,3},{2,10},{3,5},{4,12},{5,7},{6,14},{7,1},{8,16},{9,11},{... | collective-permute-start | bytes 983048 | tf_op jit(solution)/shard_map/ppermute | solution.py:592
  121.7 15.7 %collective-permute-start.33 = (f32[4,80,256]{2,1,0:T(8,128)S(1)}, f32[4,80,256]{2,1,0:T(8,128)S(1)}, u32[]{:S(2)}, u32[]{:S(2)}) collective-permute-start(f32[4,80,256]{2,1,0:T(8,128)S(1)} %get-tuple-element.99), channel_id=1, source_target_pairs={{0,24},{1,7},{2,26},{3,1},{4,28},{5,3},{6,30},{7,5},{8,0},{9,15},{... | collective-permute-start | bytes 983048 | tf_op jit(solution)/shard_map/ppermute | solution.py:592
  123.9 13.6 %collective-permute-start.34 = (f32[4,80,256]{2,1,0:T(8,128)S(1)}, f32[4,80,256]{2,1,0:T(8,128)S(1)}, u32[]{:S(2)}, u32[]{:S(2)}) collective-permute-start(f32[4,80,256]{2,1,0:T(8,128)S(1)} %get-tuple-element.100), channel_id=1, source_target_pairs={{0,16},{1,5},{2,18},{3,7},{4,20},{5,1},{6,22},{7,3},{8,24},{9,13},... | collective-permute-start | bytes 983048 | tf_op jit(solution)/shard_map/ppermute | solution.py:592
  137.5 18.6 %collective-permute-start.35 = (f32[80,256]{1,0:T(8,128)S(1)}, f32[80,256]{1,0:T(8,128)S(1)}, u32[]{:S(2)}, u32[]{:S(2)}) collective-permute-start(f32[80,256]{1,0:T(8,128)S(1)} %get-tuple-element.115), channel_id=1, source_target_pairs={{0,2},{1,9},{2,4},{3,11},{4,6},{5,13},{6,0},{7,15},{8,10},{9,17},{... | collective-permute-start | bytes 245768 | tf_op jit(solution)/shard_map/ppermute | solution.py:592
  139.6 16.5 %collective-permute-start.36 = (f32[80,256]{1,0:T(8,128)S(1)}, f32[80,256]{1,0:T(8,128)S(1)}, u32[]{:S(2)}, u32[]{:S(2)}) collective-permute-start(f32[80,256]{1,0:T(8,128)S(1)} %get-tuple-element.116), channel_id=1, source_target_pairs={{0,6},{1,25},{2,0},{3,27},{4,2},{5,29},{6,4},{7,31},{8,14},{9,1},{... | collective-permute-start | bytes 245768 | tf_op jit(solution)/shard_map/ppermute | solution.py:592
  140.8 15.3 %collective-permute-start.37 = (f32[80,256]{1,0:T(8,128)S(1)}, f32[80,256]{1,0:T(8,128)S(1)}, u32[]{:S(2)}, u32[]{:S(2)}) collective-permute-start(f32[80,256]{1,0:T(8,128)S(1)} %get-tuple-element.117), channel_id=1, source_target_pairs={{0,4},{1,17},{2,6},{3,19},{4,0},{5,21},{6,2},{7,23},{8,12},{9,25},... | collective-permute-start | bytes 245768 | tf_op jit(solution)/shard_map/ppermute | solution.py:592
  (7 other events, 29.5 us)
